TPU v7x, 32 devices: a whole 2x2x4 slice. The times are simulated.
32 devices in a mesh: section: 4 (over y, x), seq: 8 (over z, core).
Axes of the slice: x: 2, y: 2, z: 4, core: 2. Of those that a mesh axis runs over, the one named last changes fastest.
Arguments:
- hidden: bfloat16 [4096, 4096], P('seq', 'section'), may hold values from -6 to 6
- norm_gain: bfloat16 [4096], P('section'), may hold values from 0.25 to 1.75
- query_weight: bfloat16 [4096, 512], P(None, 'section')
- key_weight: bfloat16 [4096, 128], P('section')
- value_weight: bfloat16 [4096, 128], P('section'), may hold values from -0.5 to 0.5
- output_weight: bfloat16 [512, 4096], P(None, 'section'), may hold values from -0.25 to 0.25
- block_reach: int32 [32], P('seq'), may hold values from 0 to 2
- header_ids: int32 [2], replicated, may hold values from 0 to 31, as said below
Outputs:
- attention_out: bfloat16 [4096, 4096], P('seq', 'section')
Inputs may be any that keep to these rules, and one draw needn't show every extreme that they name: `header_ids`: the 2 indices are distinct block indices, and the last block, 31, is always one of them, at any position.
All inputs are finite; a program needn't handle non-finite values.
Results may differ from a plain program's by a relative error of at most 0.014.
Values may be sent and summed in bfloat16 or wider, within the bound.
A program may use at most 64 MiB of HBM per device.

v0:
```python
import math

import jax
import jax.numpy as jnp
from jax import lax
from jax.sharding import PartitionSpec as P

BLOCK = 128
REACH = 2


EPSILON = 1e-05
THETA = 500000.0


def merged(value, axis, combine):
    everything = jax.tree.map(lambda part: lax.all_gather(part, axis), value)
    leading = jax.tree.map(lambda part: part[0], everything)

    def lap(k, so_far):
        return combine(so_far, jax.tree.map(lambda part: part[k], everything))

    return lax.fori_loop(1, lax.axis_size(axis), lap, leading)


def padded(cells, sides, width):
    for axis, dim in sides:
        count = lax.axis_size(axis)
        ends = count - 1
        head = lax.slice_in_dim(cells, 0, width, axis=dim)
        tail = lax.slice_in_dim(cells, cells.shape[dim] - width, cells.shape[dim], axis=dim)
        cells = jnp.concatenate(
            [
                lax.ppermute(tail, axis, [(i, (i + 1) % count) for i in range(ends)]),
                cells,
                lax.ppermute(head, axis, [((i + 1) % count, i) for i in range(ends)]),
            ],
            axis=dim,
        )
    return cells


def tables(positions, head_width):
    middle = head_width // 2
    frequency = jnp.exp(
        -(2.0 / head_width) * math.log(THETA) * jnp.arange(middle, dtype=jnp.float32)
    )
    angles = positions.astype(jnp.float32)[:, None] * frequency[None, :]
    angles = jnp.concatenate([angles, angles], axis=1)
    return (jnp.cos(angles), jnp.sin(angles))


def rotate(values, cosine_table, sine_table):
    middle = values.shape[-1] // 2
    turned = jnp.concatenate([-values[..., middle:], values[..., :middle]], axis=-1)
    return values * cosine_table + turned * sine_table


def combine_parts(earlier, later):
    first_max, first_total, first_out = earlier
    second_max, second_total, second_out = later
    overall = jnp.maximum(first_max, second_max)
    first_factor = jnp.exp(first_max - overall)
    second_factor = jnp.exp(second_max - overall)
    return (
        overall,
        first_total * first_factor + second_total * second_factor,
        first_out * first_factor[:, None] + second_out * second_factor[:, None],
    )


def on_device(
    hidden,
    norm_gain,
    query_weight,
    key_weight,
    value_weight,
    output_weight,
    block_reach,
    header_ids,
):
    row_count = hidden.shape[0]
    part_width = hidden.shape[1]
    head_width = key_weight.shape[1]
    local_blocks = row_count // BLOCK
    total_blocks = local_blocks * lax.axis_size("seq")
    seq_place = lax.axis_index("seq")
    floats = hidden.astype(jnp.float32)
    squares = lax.psum(jnp.sum(floats * floats, axis=1), "section")
    scaling = lax.rsqrt(squares / (part_width * lax.axis_size("section")) + EPSILON)
    normed_part = (floats * scaling[:, None] * norm_gain.astype(jnp.float32)[None, :]).astype(
        jnp.bfloat16
    )
    weight_rows = query_weight
    query_sum = jnp.dot(
        lax.all_gather(normed_part, "section", axis=1, tiled=True),
        weight_rows,
        preferred_element_type=jnp.float32,
    )
    key_sum, value_sum = lax.psum(
        (
            jnp.dot(normed_part, key_weight, preferred_element_type=jnp.float32),
            jnp.dot(normed_part, value_weight, preferred_element_type=jnp.float32),
        ),
        "section",
    )
    positions = seq_place * row_count + jnp.arange(row_count, dtype=jnp.int32)
    cosine_table, sine_table = tables(positions, head_width)
    queries = rotate(query_sum, cosine_table, sine_table).astype(jnp.bfloat16)
    keys_here = rotate(key_sum, cosine_table, sine_table).astype(jnp.bfloat16)
    values_here = value_sum.astype(jnp.bfloat16)
    packed = jnp.concatenate([queries, keys_here, values_here], axis=1)
    block_numbers = seq_place * local_blocks + jnp.arange(local_blocks, dtype=jnp.int32)
    select = header_ids[:, None] == block_numbers[None, :]
    shaped = packed.reshape(local_blocks, BLOCK, 3 * head_width)
    picked = jnp.einsum(
        "hb,bre->hre", select.astype(jnp.bfloat16), shaped, preferred_element_type=jnp.float32
    )
    header_pack = lax.psum(picked, "seq").astype(jnp.bfloat16).reshape(-1, 3 * head_width)
    head_queries = header_pack[:, :head_width]
    head_keys = header_pack[:, head_width : 2 * head_width]
    head_values = header_pack[:, 2 * head_width :]
    inverse_root = 1.0 / math.sqrt(head_width)
    far_scores = (
        jnp.einsum("qd,kd->qk", head_queries, keys_here, preferred_element_type=jnp.float32)
        * inverse_root
    )
    far_max = jnp.max(far_scores, axis=1)
    far_weights = jnp.exp(far_scores - far_max[:, None])
    far_total = jnp.sum(far_weights, axis=1)
    far_out = jnp.dot(
        far_weights.astype(jnp.bfloat16), values_here, preferred_element_type=jnp.float32
    )
    merged_max, merged_total, merged_out = merged(
        (far_max, far_total, far_out), "seq", combine_parts
    )
    header_result = merged_out / merged_total[:, None]
    margin_rows = REACH * BLOCK
    stacked = jnp.concatenate([keys_here, values_here], axis=1)
    extended = padded(stacked, (("seq", 0),), margin_rows)
    near_keys = extended[:, :head_width]
    near_values = extended[:, head_width:]
    extent = row_count + 2 * margin_rows
    key_blocks = seq_place * local_blocks - REACH + jnp.arange(extent, dtype=jnp.int32) // BLOCK
    query_blocks = seq_place * local_blocks + jnp.arange(row_count, dtype=jnp.int32) // BLOCK
    limits = jnp.repeat(block_reach, BLOCK)
    key_header = jnp.any(header_ids[:, None] == key_blocks[None, :], axis=0)
    allowed = (key_blocks >= 0)[None, :] & (key_blocks < total_blocks)[None, :]
    allowed = allowed & (jnp.abs(key_blocks[None, :] - query_blocks[:, None]) <= limits[:, None])
    allowed = allowed & jnp.logical_not(key_header)[None, :]
    near_scores = (
        jnp.einsum("qd,kd->qk", queries, near_keys, preferred_element_type=jnp.float32)
        * inverse_root
    )
    near_scores = jnp.where(allowed, near_scores, -jnp.inf)
    head_scores = (
        jnp.einsum("qd,kd->qk", queries, head_keys, preferred_element_type=jnp.float32)
        * inverse_root
    )
    scores = jnp.concatenate([near_scores, head_scores], axis=1)
    row_top = jnp.max(scores, axis=1)
    weights = jnp.exp(scores - row_top[:, None])
    row_sums = jnp.sum(weights, axis=1)
    joined = jnp.concatenate([near_values, head_values], axis=0)
    mixed_out = (
        jnp.dot(weights.astype(jnp.bfloat16), joined, preferred_element_type=jnp.float32)
        / row_sums[:, None]
    )
    header_local = jnp.einsum(
        "hb,hre->bre", select.astype(jnp.float32), header_result.reshape(-1, BLOCK, head_width)
    )
    is_local_header = jnp.any(select, axis=0)
    attended = jnp.where(
        is_local_header[:, None, None],
        header_local,
        mixed_out.reshape(local_blocks, BLOCK, head_width),
    )
    attended = attended.reshape(row_count, head_width).astype(jnp.bfloat16)
    weight_rows = output_weight
    result = jnp.dot(
        lax.all_gather(attended, "section", axis=1, tiled=True),
        weight_rows,
        preferred_element_type=jnp.float32,
    )
    return result.astype(jnp.bfloat16)


def solution(mesh):
    return jax.shard_map(
        on_device,
        mesh=mesh,
        in_specs=(
            P("seq", "section"),
            P("section"),
            P(None, "section"),
            P("section", None),
            P("section", None),
            P(None, "section"),
            P("seq"),
            P(),
        ),
        out_specs=P("seq", "section"),
        check_vma=False,
    )
```

profile of v0, /device:TPU:0, one launch (start us, length us, event | category | flops | bytes accessed | tf_op | source)
XLA Modules:
  0.0 216.8 jit_solution(14717613395294858317)
XLA Ops:
  6.5 1.6 fusion.2
  8.1 11.4 %psum.28 = f32[512]{0:T(512)S(1)} all-reduce(f32[512]{0:T(512)S(1)} %fusion.2), channel_id=1, replica_groups=mesh['section'=4,'seq'=8] {'section'}, use_global_device_ids=true, to_apply=%region_2.0 | all-reduce | flops 512 | bytes 4096 | tf_op jit(solution)/shard_map/psum | solution.py:89
  19.5 0.7 convert_element_type.46
  20.2 1.6 fusion.4
  21.8 1.2 fusion.53
  23.1 0.7 all-gather.8.cloned.1.call-update
  23.9 1.7 fusion.54
  25.7 20.6 %all-reduce.5 = bf16[512,128]{0,1:T(8,128)(2,1)S(1)} all-reduce(f32[512,128]{0,1:T(8,128)S(1)} %fusion.54), channel_id=1, replica_groups=mesh['section'=4,'seq'=8] {'section'}, use_global_device_ids=true, to_apply=%region_4.0 | all-reduce | flops 65536 | bytes 393216 | tf_op jit(solution)/shard_map/psum | solution.py:100
  46.4 20.1 %all-reduce.4.cloned.1.call-done = f32[512,128]{0,1:T(8,128)} async-done(((f32[512,128]{0,1:T(8,128)}), f32[512,128]{0,1:T(8,128)}) %all-reduce.4.cloned.1.call-update) | async-done | bytes 262160 | tf_op jit(solution)/shard_map/psum | solution.py:100
  66.4 1.0 slice_negate_fusion
  67.4 53.7 %all-gather.8.cloned.1.call-done = bf16[512,4096]{1,0:T(8,128)(2,1)} async-done(((bf16[512,1024]{1,0:T(8,128)(2,1)}), bf16[512,4096]{1,0:T(8,128)(2,1)}) %all-gather.8.cloned.1.call-update) | async-done | bytes 4194320 | tf_op jit(solution)/shard_map/all_gather | solution.py:96
  121.2 3.7 %fusion.52 = f32[512,128]{0,1:T(8,128)S(1)} fusion(bf16[512,4096]{1,0:T(8,128)(2,1)} %all-gather.8.cloned.1.call-done, bf16[4096,128]{1,0:T(8,128)(2,1)S(1)} %copy-done.4), kind=kOutput, calls=%fused_computation.94 | convolution fusion | flops 536870912 | bytes 5505024 | tf_op jit(solution)/shard_map/dot_general | solution.py:95
  124.9 1.0 fusion.32
  126.8 33.2 %all-reduce.6 = bf16[2,128,384]{2,0,1:T(2,128)(2,1)S(1)} all-reduce(f32[2,128,384]{2,0,1:T(2,128)S(1)} %fusion.48), channel_id=1, replica_groups=mesh['section'=4,'seq'=8] {'seq'}, use_global_device_ids=true, to_apply=%region_5.0 | all-reduce | flops 98304 | bytes 589824 | tf_op jit(solution)/shard_map/psum | solution.py:119
  160.6 0.9 fusion.20
  161.8 8.4 %all-gather.3 = f32[8,1,256]{2,1,0:T(1,128)S(1)} all-gather(f32[1,1,256]{2,1,0:T(1,128)S(1)} %bitcast.66), channel_id=2, replica_groups=mesh['section'=4,'seq'=8] {'seq'}, dimensions={0}, use_global_device_ids=true | all-gather | bytes 9216 | tf_op jit(solution)/shard_map/all_gather | solution.py:17
  170.4 10.4 %all-gather.4 = f32[8,1,256]{2,1,0:T(1,128)S(1)} all-gather(f32[1,1,256]{2,1,0:T(1,128)S(1)} %bitcast.67), channel_id=3, replica_groups=mesh['section'=4,'seq'=8] {'seq'}, dimensions={0}, use_global_device_ids=true | all-gather | bytes 9216 | tf_op jit(solution)/shard_map/all_gather | solution.py:17
  180.9 2.2 %collective-permute-start = (bf16[256,256]{0,1:T(8,128)(2,1)S(1)}, bf16[256,256]{0,1:T(8,128)(2,1)S(1)}, u32[]{:S(2)}, u32[]{:S(2)}) collective-permute-start(bf16[256,256]{0,1:T(8,128)(2,1)S(1)} %get-tuple-element.204), channel_id=1, source_target_pairs={{0,1},{1,2},{2,3},{3,4},{4,5},{5,6},{6,7},{8,9},{9,10},{10,11},{11... | collective-permute-start | bytes 393224 | tf_op jit(solution)/shard_map/ppermute | solution.py:34
  183.1 1.3 collective-permute-start.1
  184.8 1.6 collective-permute-done.1
  186.4 1.0 fusion.49
  189.1 0.9 slice.68
  190.0 7.9 %while.19 = (s32[]{:T(128)}, f32[256]{0:T(256)S(1)}, f32[256]{0:T(256)S(1)}, f32[256,128]{1,0:T(8,128)S(1)}, f32[8,256]{1,0:T(8,128)S(1)}, /*index=5*/f32[8,256]...) while((s32[]{:T(128)}, f32[256]{0:T(256)S(1)}, f32[256]{0:T(256)S(1)}, ...), condition=%wide.region_9.10_spmd, body=%wide.region_8.0_spmd.sunk | while | flops 99845 | bytes 407695 | solution.py:23
  190.1 1.1 fusion.69
  191.2 1.1 fusion.69
  192.3 1.1 fusion.69
  193.5 1.1 fusion.69
  194.6 1.1 fusion.69
  195.7 1.1 fusion.69
  196.9 1.1 fusion.69
  198.4 10.2 %all_gather.31 = bf16[512,512]{1,0:T(8,128)(2,1)S(1)} all-gather(bf16[512,128]{1,0:T(8,128)(2,1)S(1)} %bitcast.58), channel_id=1, replica_groups=mesh['section'=4,'seq'=8] {'section'}, dimensions={1}, use_global_device_ids=true | all-gather | bytes 655360 | tf_op jit(solution)/shard_map/all_gather | solution.py:181
  208.6 1.7 convolution_convert_fusion
  (82 shorter events, 4.9 us)
Async XLA Ops:
  6.5 202.1 %copy-start = (bf16[512,1024]{1,0:T(8,128)(2,1)S(1)}, bf16[512,1024]{1,0:T(8,128)(2,1)}, u32[]{:S(2)}) copy-start(bf16[512,1024]{1,0:T(8,128)(2,1)} %param.15) | copy-start | bytes 3145732
  6.5 15.3 %copy-start.5 = (bf16[1024,128]{1,0:T(8,128)(2,1)S(1)}, bf16[1024,128]{1,0:T(8,128)(2,1)}, u32[]{:S(2)}) copy-start(bf16[1024,128]{1,0:T(8,128)(2,1)} %param.13) | copy-start | bytes 786436
  6.5 59.9 %all-reduce.4.cloned.1.call-start = ((), (), s32[]{:S(2)}) async-start(), calls=%async_computation.1 | async-start | bytes 524288 | tf_op jit(solution)/shard_map/psum | solution.py:100
  20.2 3.6 %copy-start.6 = (bf16[1024,128]{1,0:T(8,128)(2,1)S(1)}, bf16[1024,128]{1,0:T(8,128)(2,1)}, u32[]{:S(2)}) copy-start(bf16[1024,128]{1,0:T(8,128)(2,1)} %param.14) | copy-start | bytes 786436
  21.8 1.3 copy-start.1
  21.8 3.8 %copy-start.9 = (s32[2]{0:T(128)S(1)}, s32[2]{0:T(128)}, u32[]{:S(2)}) copy-start(s32[2]{0:T(128)} %param.17) | copy-start | bytes 28
  23.0 98.1 %copy-start.4 = (bf16[4096,128]{1,0:T(8,128)(2,1)S(1)}, bf16[4096,128]{1,0:T(8,128)(2,1)}, u32[]{:S(2)}) copy-start(bf16[4096,128]{1,0:T(8,128)(2,1)} %param.12) | copy-start | bytes 3145732
  23.0 98.1 %all-gather.8.cloned.1.call-start = ((), (), s32[]{:S(2)}) async-start(), calls=%async_computation | async-start | bytes 5242880 | tf_op jit(solution)/shard_map/all_gather | solution.py:96
  23.8 165.3 %all-gather.10.cloned.1.call-start = ((), (), s32[]{:S(2)}) async-start(), calls=%async_computation.2 | async-start | bytes 1179648 | tf_op jit(solution)/shard_map/all_gather | solution.py:17
  67.4 57.5 %copy-start.3 = (f32[512,128]{0,1:T(8,128)S(1)}, f32[512,128]{0,1:T(8,128)}, u32[]{:S(2)}) copy-start(f32[512,128]{0,1:T(8,128)} %all-reduce.4.cloned.1.call-done) | copy-start | bytes 786436
  126.4 35.3 %copy-start.10 = (s32[4]{0:T(128)S(1)}, s32[4]{0:T(128)}, u32[]{:S(2)}) copy-start(s32[4]{0:T(128)} %param.16) | copy-start | bytes 52
  170.2 17.3 %copy-start.8 = (f32[8,1,256]{2,1,0:T(1,128)}, f32[8,1,256]{2,1,0:T(1,128)S(1)}, u32[]{:S(2)}) copy-start(f32[8,1,256]{2,1,0:T(1,128)S(1)} %all-gather.3) | copy-start | bytes 24580
  180.9 6.6 %copy-start.7 = (f32[8,1,256]{2,1,0:T(1,128)}, f32[8,1,256]{2,1,0:T(1,128)S(1)}, u32[]{:S(2)}) copy-start(f32[8,1,256]{2,1,0:T(1,128)S(1)} %all-gather.4) | copy-start | bytes 24580
  180.9 3.9 %collective-permute-start = (bf16[256,256]{0,1:T(8,128)(2,1)S(1)}, bf16[256,256]{0,1:T(8,128)(2,1)S(1)}, u32[]{:S(2)}, u32[]{:S(2)}) collective-permute-start(bf16[256,256]{0,1:T(8,128)(2,1)S(1)} %get-tuple-element.204), channel_id=1, source_target_pairs={{0,1},{1,2},{2,3},{3,4},{4,5},{5,6},{6,7},{8,9},{9,10},{10,11},{11... | collective-permute-start | bytes 393224 | tf_op jit(solution)/shard_map/ppermute | solution.py:34
  183.1 3.2 %collective-permute-start.1 = (bf16[256,256]{0,1:T(8,128)(2,1)S(1)}, bf16[256,256]{0,1:T(8,128)(2,1)S(1)}, u32[]{:S(2)}, u32[]{:S(2)}) collective-permute-start(bf16[256,256]{0,1:T(8,128)(2,1)S(1)} %get-tuple-element.205), channel_id=1, source_target_pairs={{1,0},{2,1},{3,2},{4,3},{5,4},{6,5},{7,6},{9,8},{10,9},{11,10},{12... | collective-permute-start | bytes 393224 | tf_op jit(solution)/shard_map/ppermute | solution.py:36
  186.4 1.1 copy-start.2
  187.5 1.0 slice-start
  188.5 1.5 slice-start.1
  188.5 1.5 slice-start.2
Sparse Core Ops, SparseCore 0:
  23.2 43.2 all-reduce.3
  68.4 52.6 all-gather.7
  161.7 19.3 all-gather.9
where the time goes:
time: 218 us; the launch traced here: 217 us
  blocking collectives  94.1 us (43%)
  waiting for transfers between devices  76.1 us (35%)
  other arithmetic  14.8 us (7%)
  between operations  13.5 us (6%)
  matrix products  12.3 us (6%)
  starting transfers between devices  3.61 us (2%)
  local copies, waits for them, and re-layouts  2.22 us (1%)
    all_gather x1, waiting for transfers between devices, on_device(): lax.all_gather(normed_part, 'section', axis=1, tiled=True)  53.7 us
    psum x1, blocking collectives, on_device(): lax.psum(picked, 'seq').astype(jnp.bfloat16).reshape(-1, 3 * head_width)  33.2 us
    psum x1, blocking collectives, on_device(): lax.psum((jnp.dot(normed_part, key_weight, preferred_element_type=jnp.flo...  20.6 us
    psum x1, waiting for transfers between devices, on_device(): lax.psum((jnp.dot(normed_part, key_weight, preferred_element_type=jnp.flo...  20.1 us
    all_gather x2, blocking collectives, merged(): everything = jax.tree.map(lambda part: lax.all_gather(part, axis), value)  18.8 us
    psum x1, blocking collectives, on_device(): squares = lax.psum(jnp.sum(floats * floats, axis=1), 'section')  11.4 us
    all_gather x1, blocking collectives, on_device(): lax.all_gather(attended, 'section', axis=1, tiled=True)  10.2 us
    add x7, other arithmetic, combine_parts(): first_out * first_factor[:, None] + second_out * second_factor[:, None]  7.5 us
  transfers between devices with their start and end apart: 5, of which 3 were waited for; matrix products, arithmetic and copies ran while one was open for 3% of the time, Pallas kernels for 0%

commit v1 on v0

--- a/solution.py
+++ b/solution.py
@@ -1,8 +1,11 @@
+import functools
 import math
 
 import jax
 import jax.numpy as jnp
 from jax import lax
+from jax.experimental import pallas as pl
+from jax.experimental.pallas import tpu as pltpu
 from jax.sharding import PartitionSpec as P
 
 BLOCK = 128
@@ -185,9 +188,368 @@
     return result.astype(jnp.bfloat16)
 
 
+MESH = pl.DeviceIdType.MESH
+LOW = -1e30
+FUSED_BLOCKS = 64
+
+
+def fused(
+    n_section,
+    n_line,
+    hidden_ref,
+    gain_ref,
+    query_ref,
+    key_ref,
+    value_ref,
+    cos_ref,
+    sin_ref,
+    reach_ref,
+    ids_ref,
+    out_ref,
+    x,
+    normed,
+    wq,
+    wkv,
+    squares,
+    kv_part,
+    kv_got,
+    q_part,
+    q_got,
+    blocks,
+    queries,
+    top,
+    total,
+    acc,
+    local_sem,
+    w_send,
+    w_recv,
+    wf_send,
+    wf_recv,
+    sq_send,
+    sq_recv,
+    kv_send,
+    kv_recv,
+    q_send,
+    q_recv,
+    line_send,
+    plane_send,
+    twin_send,
+    block_recv,
+    out_send,
+    out_recv,
+):
+    width = x.shape[1]
+    half = width // 2
+    head = wq.shape[2]
+    s = lax.axis_index("section")
+    j = lax.axis_index("seq")
+    z = j // 2
+    c = j % 2
+    twin = z * 2 + (1 - c)
+    others = [(s + k) % n_section for k in range(1, n_section)]
+    line = [((z + k) % n_line) * 2 + c for k in range(1, n_line)]
+
+    def push(src, dst, send, recv, section, seq):
+        copy = pltpu.make_async_remote_copy(
+            src_ref=src,
+            dst_ref=dst,
+            send_sem=send,
+            recv_sem=recv,
+            device_id=(section, seq),
+            device_id_type=MESH,
+        )
+        copy.start()
+        pending.append(copy)
+
+    def arrived(dst, recv):
+        pltpu.make_async_remote_copy(
+            src_ref=dst,
+            dst_ref=dst,
+            send_sem=local_sem.at[4],
+            recv_sem=recv,
+            device_id=(s, twin),
+            device_id_type=MESH,
+        ).wait_recv()
+
+    pending = []
+    get_x = pltpu.make_async_copy(hidden_ref, x, local_sem.at[0])
+    get_k = pltpu.make_async_copy(key_ref, wkv.at[:, 0:head], local_sem.at[1])
+    get_v = pltpu.make_async_copy(value_ref, wkv.at[:, head : 2 * head], local_sem.at[2])
+    get_q = pltpu.make_async_copy(
+        query_ref.at[pl.ds(pl.multiple_of(s * width, width), width), :], wq.at[s], local_sem.at[3]
+    )
+    get_x.start()
+    get_k.start()
+    get_v.start()
+    get_q.start()
+
+    barrier = pltpu.get_barrier_semaphore()
+    friends = [(t, j) for t in others] + [(s, i) for i in line] + [(s, twin)]
+    for friend in friends:
+        pl.semaphore_signal(barrier, inc=1, device_id=friend, device_id_type=MESH)
+    pl.semaphore_wait(barrier, len(friends))
+
+    mine = pl.ds(pl.multiple_of(c * half, half), half)
+    for k, t in enumerate(others):
+        push(
+            query_ref.at[pl.ds(pl.multiple_of(t * width + c * half, half), half), :],
+            wq.at[s, mine, :],
+            w_send.at[k],
+            w_recv.at[s],
+            t,
+            j,
+        )
+
+    get_x.wait()
+    for r in range(n_section):
+        part = x[r * BLOCK : (r + 1) * BLOCK, :].astype(jnp.float32)
+        column = jnp.sum(part * part, axis=1, keepdims=True)
+        squares[s, r] = jnp.transpose(jnp.broadcast_to(column, (BLOCK, BLOCK)))[:8, :]
+    for k, t in enumerate(others):
+        push(squares.at[s], squares.at[s], sq_send.at[k], sq_recv.at[s], t, j)
+    for t in others:
+        arrived(squares.at[t], sq_recv.at[t])
+    sums = squares[0]
+    for t in range(1, n_section):
+        sums = sums + squares[t]
+    scaling = lax.rsqrt(sums / (width * n_section) + EPSILON)
+    gain = gain_ref[...].astype(jnp.float32)
+    for r in range(n_section):
+        column = jnp.transpose(jnp.broadcast_to(scaling[r, 0:1, :], (BLOCK, BLOCK)))[:, 0:1]
+        part = x[r * BLOCK : (r + 1) * BLOCK, :].astype(jnp.float32)
+        normed[r * BLOCK : (r + 1) * BLOCK, :] = (part * column * gain).astype(jnp.bfloat16)
+
+    get_k.wait()
+    get_v.wait()
+    kv_part[...] = (
+        jnp.dot(normed[...], wkv[...], preferred_element_type=jnp.float32)
+        .astype(jnp.bfloat16)
+        .reshape(kv_part.shape)
+    )
+    for k, t in enumerate(others):
+        push(kv_part.at[t], kv_got.at[s], kv_send.at[k], kv_recv.at[s], t, j)
+
+    def project(k):
+        owner = (s + k) % n_section
+        q_part[k] = (
+            jnp.dot(normed[...], wq[owner], preferred_element_type=jnp.float32)
+            .astype(jnp.bfloat16)
+            .reshape(q_part.shape[1:])
+        )
+        for i, t in enumerate(others):
+            push(q_part.at[k, t], q_got.at[s, owner], q_send.at[k, i], q_recv.at[s, owner], t, j)
+
+    get_q.wait()
+    project(0)
+
+    cosine = cos_ref[...]
+    sine = sin_ref[...]
+
+    def turned(values):
+        return values * cosine + pltpu.roll(values, head // 2, axis=1) * sine
+
+    b = j * n_section + s
+    for t in others:
+        arrived(kv_got.at[t], kv_recv.at[t])
+    kv = kv_part[s].astype(jnp.float32)
+    for t in others:
+        kv = kv + kv_got[t].astype(jnp.float32)
+    blocks[b, :, 0:head] = turned(kv[:, :head]).astype(jnp.bfloat16)
+    blocks[b, :, head : 2 * head] = kv[:, head:].astype(jnp.bfloat16)
+
+    def spread(number, slot):
+        for k, t in enumerate(others):
+            push(
+                blocks.at[number],
+                blocks.at[number],
+                plane_send.at[slot, k],
+                block_recv.at[number],
+                t,
+                j,
+            )
+        push(
+            blocks.at[number], blocks.at[number], twin_send.at[slot, 0], block_recv.at[number], s, twin
+        )
+
+    for k, i in enumerate(line):
+        push(blocks.at[b], blocks.at[b], line_send.at[k], block_recv.at[b], s, i)
+    spread(b, 0)
+
+    for k, t in enumerate(others):
+        arrived(wq.at[t, mine, :], w_recv.at[t])
+        push(wq.at[t, mine, :], wq.at[t, mine, :], wf_send.at[k], wf_recv.at[t], s, twin)
+    theirs = pl.ds(pl.multiple_of((1 - c) * half, half), half)
+    for k, t in enumerate(others):
+        arrived(wq.at[t, theirs, :], wf_recv.at[t])
+        project(k + 1)
+
+    for k, i in enumerate(line):
+        number = i * n_section + s
+        arrived(blocks.at[number], block_recv.at[number])
+        spread(number, k + 1)
+
+    for t in others:
+        for h in range(n_section):
+            arrived(q_got.at[t, h], q_recv.at[t, h])
+    for h in range(n_section):
+        place = (h + n_section - s) % n_section
+        value = q_part[place, s].astype(jnp.float32)
+        for t in others:
+            value = value + q_got[t, h].astype(jnp.float32)
+        queries[h] = turned(value).astype(jnp.bfloat16)
+
+    first = ids_ref[0]
+    second = ids_ref[1]
+    own_header = jnp.logical_or(first == b, second == b)
+    limit = jnp.where(own_header, n_section * n_line * 2, reach_ref[s])
+    group = n_section * BLOCK
+    factor = 1.4426950408889634 / math.sqrt(head)
+    top[...] = jnp.full(top.shape, LOW, jnp.float32)
+    total[...] = jnp.zeros(total.shape, jnp.float32)
+    acc[...] = jnp.zeros(acc.shape, jnp.float32)
+
+    def attend(seq):
+        start = seq * n_section
+        numbers = start + lax.broadcasted_iota(jnp.int32, (1, group), 1) // BLOCK
+        valid = (numbers == first) | (numbers == second) | (jnp.abs(numbers - b) <= limit)
+        bias = jnp.where(valid, 0.0, LOW)
+        keys = blocks[pl.ds(start, n_section), :, 0:head].reshape(group, head)
+        values = blocks[pl.ds(start, n_section), :, head : 2 * head].reshape(group, head)
+        for h in range(n_section):
+            scores = lax.dot_general(
+                queries[h], keys, (((1,), (1,)), ((), ())), preferred_element_type=jnp.float32
+            )
+            scores = scores * factor + bias
+            before = top[h]
+            after = jnp.maximum(before, jnp.max(scores, axis=1, keepdims=True))
+            fade = jnp.exp2(before - after)
+            weights = jnp.exp2(scores - after[:, 0:1])
+            top[h] = after
+            total[h] = total[h] * fade + jnp.sum(weights, axis=1, keepdims=True)
+            acc[h] = acc[h] * fade + jnp.dot(
+                weights.astype(jnp.bfloat16), values, preferred_element_type=jnp.float32
+            )
+
+    for i in range(n_line):
+        seq = ((z + i) % n_line) * 2 + c
+        for k, t in enumerate(others):
+            number = seq * n_section + t
+            arrived(blocks.at[number], block_recv.at[number])
+            push(
+                blocks.at[number],
+                blocks.at[number],
+                twin_send.at[i, k + 1],
+                block_recv.at[number],
+                s,
+                twin,
+            )
+        attend(seq)
+    for i in range(n_line):
+        seq = ((z + i) % n_line) * 2 + (1 - c)
+        for t in range(n_section):
+            arrived(blocks.at[seq * n_section + t], block_recv.at[seq * n_section + t])
+        attend(seq)
+
+    for h in range(n_section):
+        out_ref[s, :, h * head : (h + 1) * head] = (acc[h] / total[h]).astype(jnp.bfloat16)
+    for k, t in enumerate(others):
+        push(out_ref.at[s], out_ref.at[s], out_send.at[k], out_recv.at[s], t, j)
+    for t in others:
+        arrived(out_ref.at[t], out_recv.at[t])
+    for copy in pending:
+        copy.wait_send()
+
+
+def on_device_fused(
+    n_section,
+    n_seq,
+    hidden,
+    norm_gain,
+    query_weight,
+    key_weight,
+    value_weight,
+    output_weight,
+    block_reach,
+    header_ids,
+):
+    rows, width = hidden.shape
+    head = key_weight.shape[1]
+    n_line = n_seq // 2
+    n_blocks = n_section * n_seq
+    first = lax.axis_index("seq") * rows + lax.axis_index("section") * BLOCK
+    cosine, sine = tables(first + jnp.arange(BLOCK, dtype=jnp.int32), head)
+    sine = jnp.concatenate([-sine[:, : head // 2], sine[:, head // 2 :]], axis=1)
+    vmem = pl.BlockSpec(memory_space=pltpu.VMEM)
+    smem = pl.BlockSpec(memory_space=pltpu.SMEM)
+    anywhere = pl.BlockSpec(memory_space=pl.ANY)
+    dma = pltpu.SemaphoreType.DMA
+    bf16 = jnp.bfloat16
+    f32 = jnp.float32
+    attended = pl.pallas_call(
+        functools.partial(fused, n_section, n_line),
+        out_shape=jax.ShapeDtypeStruct((n_section, BLOCK, n_section * head), bf16),
+        in_specs=[anywhere, vmem, anywhere, anywhere, anywhere, vmem, vmem, smem, smem],
+        out_specs=vmem,
+        scratch_shapes=[
+            pltpu.VMEM((rows, width), bf16),
+            pltpu.VMEM((rows, width), bf16),
+            pltpu.VMEM((n_section, width, head), bf16),
+            pltpu.VMEM((width, 2 * head), bf16),
+            pltpu.VMEM((n_section, n_section, 8, BLOCK), f32),
+            pltpu.VMEM((n_section, BLOCK, 2 * head), bf16),
+            pltpu.VMEM((n_section, BLOCK, 2 * head), bf16),
+            pltpu.VMEM((n_section, n_section, BLOCK, head), bf16),
+            pltpu.VMEM((n_section, n_section, BLOCK, head), bf16),
+            pltpu.VMEM((n_blocks, BLOCK, 2 * head), bf16),
+            pltpu.VMEM((n_section, BLOCK, head), bf16),
+            pltpu.VMEM((n_section, BLOCK, head), f32),
+            pltpu.VMEM((n_section, BLOCK, head), f32),
+            pltpu.VMEM((n_section, BLOCK, head), f32),
+            dma((5,)),
+            dma((n_section - 1,)),
+            dma((n_section,)),
+            dma((n_section - 1,)),
+            dma((n_section,)),
+            dma((n_section - 1,)),
+            dma((n_section,)),
+            dma((n_section - 1,)),
+            dma((n_section,)),
+            dma((n_section, n_section - 1)),
+            dma((n_section, n_section)),
+            dma((n_line - 1,)),
+            dma((n_line, n_section - 1)),
+            dma((n_line, n_section)),
+            dma((n_blocks,)),
+            dma((n_section - 1,)),
+            dma((n_section,)),
+        ],
+        compiler_params=pltpu.CompilerParams(
+            collective_id=0, has_side_effects=True, vmem_limit_bytes=40 * 1024 * 1024
+        ),
+    )(
+        hidden,
+        norm_gain.reshape(1, width),
+        query_weight,
+        key_weight,
+        value_weight,
+        cosine,
+        sine,
+        block_reach,
+        header_ids,
+    )
+    return jnp.dot(
+        attended.reshape(rows, n_section * head), output_weight, preferred_element_type=f32
+    ).astype(bf16)
+
+
 def solution(mesh):
+    n_section, n_seq = mesh.shape["section"], mesh.shape["seq"]
+    if n_section * n_seq <= FUSED_BLOCKS:
+        program = functools.partial(on_device_fused, n_section, n_seq)
+    else:
+        program = on_device
     return jax.shard_map(
-        on_device,
+        program,
         mesh=mesh,
         in_specs=(
             P("seq", "section"),

time: 218 us -> 62.8 us (0.29)
  blocking collectives: 94.1 us -> 0 us
  waiting for transfers between devices: 76.1 us -> 0 us
  Pallas kernels: 0 us -> 53.7 us
  other arithmetic: 14.8 us -> 0.57 us
  between operations: 13.5 us -> 0.06 us
  matrix products: 12.3 us -> 1.71 us
  local copies, waits for them, and re-layouts: 2.22 us -> 6.43 us
  starting transfers between devices: 3.61 us -> 0 us
    psum x3 -> x0, blocking collectives: 65.1 us -> none  [the longest x1 33.2 us: on_device(): lax.psum(picked, 'seq').astype(jnp.bfloat16).reshape(-1, 3 * head_width)]
    all_gather x2 -> x0, waiting for transfers between devices: 53.7 us -> none  [the longest x1 53.7 us: on_device(): lax.all_gather(normed_part, 'section', axis=1, tiled=True)]
    pallas_call x0 -> x1, Pallas kernels: none -> 53.7 us  [on_device_fused(): pl.pallas_call(functools.partial(fused, n_section, n_line), out_shape=jax...]
    all_gather x3 -> x0, blocking collectives: 29 us -> none  [the longest x2 18.8 us: merged(): everything = jax.tree.map(lambda part: lax.all_gather(part, axis), value)]
    psum x1 -> x0, waiting for transfers between devices: 20.1 us -> none  [on_device(): lax.psum((jnp.dot(normed_part, key_weight, preferred_element_type=jnp.flo...]
    dot_general x11 -> x1, matrix products: 12.3 us -> 1.71 us  [on_device_fused(): jnp.dot(attended.reshape(rows, n_section * head), output_weight, preferre...]
    add x17 -> x0, other arithmetic: 7.66 us -> none  [the longest x7 7.5 us: combine_parts(): first_out * first_factor[:, None] + second_out * second_factor[:, None]]
    unnamed x25 -> x14, local copies, waits for them, and re-layouts: 0.08 us -> 5.66 us
  transfers between devices with their start and end apart: 5 -> 0, of which waited for: 3 -> 0; matrix products, arithmetic and copies ran while one was open for 3% -> 0% of each run, Pallas kernels for 0% -> 0%
where the time goes in v1:
time: 62.8 us; the launch traced here: 62.5 us
  Pallas kernels  53.7 us (86%)
  local copies, waits for them, and re-layouts  6.43 us (10%)
  matrix products  1.71 us (3%)
    pallas_call x1, Pallas kernels, on_device_fused(): pl.pallas_call(functools.partial(fused, n_section, n_line), out_shape=jax...  53.7 us
    unnamed x14, local copies, waits for them, and re-layouts  5.66 us
    dot_general x1, matrix products, on_device_fused(): jnp.dot(attended.reshape(rows, n_section * head), output_weight, preferre...  1.71 us

profile of v1, /device:TPU:0, one launch (start us, length us, event | category | flops | bytes accessed | tf_op | source)
XLA Modules:
  0.0 62.5 jit_solution(3576731080222513710)
XLA Ops:
  0.0 0.0 copy-start
  0.0 0.8 %reshape.16.gain_ref = bf16[1,1024]{1,0:T(2,128)(2,1)S(1)} reshape(bf16[1024]{0:T(1024)(128)(2,1)} %param.9) | data formatting | bytes 4096 | tf_op jit(solution)/shard_map/reshape | solution.py:531
  0.8 0.1 broadcast_multiply_fusion
  0.9 0.3 fusion
  1.2 0.1 slice_negate_fusion
  1.3 0.1 pad_maximum_fusion.1.sin_ref
  1.4 0.0 copy-start.1
  1.4 1.2 %copy-done.1 = bf16[512,1024]{1,0:T(8,128)(2,1)S(1)} copy-done((bf16[512,1024]{1,0:T(8,128)(2,1)S(1)}, bf16[512,1024]{1,0:T(8,128)(2,1)}, u32[]{:S(2)}) %copy-start.1) | copy-done | bytes 1048600
  2.6 0.0 copy-start.2
  2.6 1.2 %copy-done.2 = bf16[4096,128]{1,0:T(8,128)(2,1)S(1)} copy-done((bf16[4096,128]{1,0:T(8,128)(2,1)S(1)}, bf16[4096,128]{1,0:T(8,128)(2,1)}, u32[]{:S(2)}) %copy-start.2) | copy-done | bytes 1048600
  3.8 0.0 copy-start.3
  3.8 0.9 %copy-done.3 = bf16[1024,128]{1,0:T(8,128)(2,1)S(1)} copy-done((bf16[1024,128]{1,0:T(8,128)(2,1)S(1)}, bf16[1024,128]{1,0:T(8,128)(2,1)}, u32[]{:S(2)}) %copy-start.3) | copy-done | bytes 262168
  4.8 0.0 copy-start.4
  4.8 0.9 %copy-done.4 = bf16[1024,128]{1,0:T(8,128)(2,1)S(1)} copy-done((bf16[1024,128]{1,0:T(8,128)(2,1)S(1)}, bf16[1024,128]{1,0:T(8,128)(2,1)}, u32[]{:S(2)}) %copy-start.4) | copy-done | bytes 262168
  5.7 0.0 copy-start.5
  5.7 0.7 %copy-done.5 = s32[4]{0:T(128)S(1)} copy-done((s32[4]{0:T(128)S(1)}, s32[4]{0:T(128)}, u32[]{:S(2)}) %copy-start.5) | copy-done | bytes 40
  6.4 0.0 copy-start.6
  6.4 0.7 %copy-done.6 = s32[2]{0:T(128)S(1)} copy-done((s32[2]{0:T(128)S(1)}, s32[2]{0:T(128)}, u32[]{:S(2)}) %copy-start.6) | copy-done | bytes 32
  7.0 53.7 %shard_map.82 = bf16[4,128,512]{2,1,0:T(8,128)(2,1)S(1)} custom-call(bf16[512,1024]{1,0:T(8,128)(2,1)S(1)} %copy-done.1, bf16[1,1024]{1,0:T(2,128)(2,1)S(1)} %reshape.16.gain_ref, bf16[4096,128]{1,0:T(8,128)(2,1)S(1)} %copy-done.2, bf16[1024,128]{1,0:T(8,128)(2,1)S(1)} %copy-done.3, bf16[1024,128]{1,0:T(8,128)(2,1)S(1)} %copy-done.4, ...), custom_call_target="tpu_custom_call" | custom-call | tf_op jit(solution)/shard_map/pallas_call | solution.py:488
  60.8 0.0 copy-done
  60.8 1.7 %convolution_convert_fusion = bf16[512,1024]{1,0:T(8,128)(2,1)} fusion(bf16[512,512]{1,0:T(8,128)(2,1)S(1)} %bitcast.3, bf16[512,1024]{1,0:T(8,128)(2,1)S(1)} %copy-done), kind=kOutput, calls=%fused_computation | convolution fusion | flops 537395200 | bytes 2621440 | tf_op jit(solution)/shard_map/dot_general | solution.py:540
  (2 shorter events, 0.0 us)
Async XLA Ops:
  0.0 60.8 %copy-start = (bf16[512,1024]{1,0:T(8,128)(2,1)S(1)}, bf16[512,1024]{1,0:T(8,128)(2,1)}, u32[]{:S(2)}) copy-start(bf16[512,1024]{1,0:T(8,128)(2,1)} %param.13) | copy-start | bytes 3145732
  1.4 1.2 %copy-start.1 = (bf16[512,1024]{1,0:T(8,128)(2,1)S(1)}, bf16[512,1024]{1,0:T(8,128)(2,1)}, u32[]{:S(2)}) copy-start(bf16[512,1024]{1,0:T(8,128)(2,1)} %hidden_ref.1) | copy-start | bytes 3145732
  2.6 1.2 %copy-start.2 = (bf16[4096,128]{1,0:T(8,128)(2,1)S(1)}, bf16[4096,128]{1,0:T(8,128)(2,1)}, u32[]{:S(2)}) copy-start(bf16[4096,128]{1,0:T(8,128)(2,1)} %query_ref.1) | copy-start | bytes 3145732
  3.8 0.9 %copy-start.3 = (bf16[1024,128]{1,0:T(8,128)(2,1)S(1)}, bf16[1024,128]{1,0:T(8,128)(2,1)}, u32[]{:S(2)}) copy-start(bf16[1024,128]{1,0:T(8,128)(2,1)} %key_ref.1) | copy-start | bytes 786436
  4.8 0.9 %copy-start.4 = (bf16[1024,128]{1,0:T(8,128)(2,1)S(1)}, bf16[1024,128]{1,0:T(8,128)(2,1)}, u32[]{:S(2)}) copy-start(bf16[1024,128]{1,0:T(8,128)(2,1)} %value_ref.1) | copy-start | bytes 786436
  5.7 0.7 %copy-start.5 = (s32[4]{0:T(128)S(1)}, s32[4]{0:T(128)}, u32[]{:S(2)}) copy-start(s32[4]{0:T(128)} %reach_ref.1) | copy-start | bytes 52
  6.4 0.7 %copy-start.6 = (s32[2]{0:T(128)S(1)}, s32[2]{0:T(128)}, u32[]{:S(2)}) copy-start(s32[2]{0:T(128)} %ids_ref.1) | copy-start | bytes 28

commit v2 on v1

--- a/solution.py
+++ b/solution.py
@@ -201,8 +201,6 @@
     query_ref,
     key_ref,
     value_ref,
-    cos_ref,
-    sin_ref,
     reach_ref,
     ids_ref,
     out_ref,
@@ -221,6 +219,7 @@
     total,
     acc,
     local_sem,
+    x_sem,
     w_send,
     w_recv,
     wf_send,
@@ -272,13 +271,16 @@
         ).wait_recv()
 
     pending = []
-    get_x = pltpu.make_async_copy(hidden_ref, x, local_sem.at[0])
+    get_x = []
+    for r in range(n_section):
+        rows = pl.ds(r * BLOCK, BLOCK)
+        get_x.append(pltpu.make_async_copy(hidden_ref.at[rows, :], x.at[rows, :], x_sem.at[r]))
+        get_x[r].start()
     get_k = pltpu.make_async_copy(key_ref, wkv.at[:, 0:head], local_sem.at[1])
     get_v = pltpu.make_async_copy(value_ref, wkv.at[:, head : 2 * head], local_sem.at[2])
     get_q = pltpu.make_async_copy(
         query_ref.at[pl.ds(pl.multiple_of(s * width, width), width), :], wq.at[s], local_sem.at[3]
     )
-    get_x.start()
     get_k.start()
     get_v.start()
     get_q.start()
@@ -300,8 +302,16 @@
             j,
         )
 
-    get_x.wait()
+    b = j * n_section + s
+    lanes = lax.broadcasted_iota(jnp.int32, (BLOCK, head), 1)
+    positions = b * BLOCK + lax.broadcasted_iota(jnp.int32, (BLOCK, head), 0)
+    spots = lax.rem(lanes, head // 2).astype(jnp.float32)
+    angles = positions.astype(jnp.float32) * jnp.exp(-(2.0 / head) * math.log(THETA) * spots)
+    cosine = jnp.cos(angles)
+    sine = jnp.where(lanes < head // 2, -1.0, 1.0) * jnp.sin(angles)
+
     for r in range(n_section):
+        get_x[r].wait()
         part = x[r * BLOCK : (r + 1) * BLOCK, :].astype(jnp.float32)
         column = jnp.sum(part * part, axis=1, keepdims=True)
         squares[s, r] = jnp.transpose(jnp.broadcast_to(column, (BLOCK, BLOCK)))[:8, :]
@@ -313,7 +323,7 @@
     for t in range(1, n_section):
         sums = sums + squares[t]
     scaling = lax.rsqrt(sums / (width * n_section) + EPSILON)
-    gain = gain_ref[...].astype(jnp.float32)
+    gain = gain_ref[...].astype(jnp.float32).reshape(1, width)
     for r in range(n_section):
         column = jnp.transpose(jnp.broadcast_to(scaling[r, 0:1, :], (BLOCK, BLOCK)))[:, 0:1]
         part = x[r * BLOCK : (r + 1) * BLOCK, :].astype(jnp.float32)
@@ -341,14 +351,13 @@
 
     get_q.wait()
     project(0)
-
-    cosine = cos_ref[...]
-    sine = sin_ref[...]
+    for k, t in enumerate(others):
+        arrived(wq.at[t, mine, :], w_recv.at[t])
+        push(wq.at[t, mine, :], wq.at[t, mine, :], wf_send.at[k], wf_recv.at[t], s, twin)
 
     def turned(values):
         return values * cosine + pltpu.roll(values, head // 2, axis=1) * sine
 
-    b = j * n_section + s
     for t in others:
         arrived(kv_got.at[t], kv_recv.at[t])
     kv = kv_part[s].astype(jnp.float32)
@@ -357,27 +366,24 @@
     blocks[b, :, 0:head] = turned(kv[:, :head]).astype(jnp.bfloat16)
     blocks[b, :, head : 2 * head] = kv[:, head:].astype(jnp.bfloat16)
 
+    across = s + 1 - 2 * (s % 2)
+    along = (s + 2) % n_section
+    corner = (across + 2) % n_section
+    relayed = jnp.where(c == 0, across, along)
+    direct = jnp.where(c == 0, along, across)
+
+    def hand(number, send, section, seq):
+        push(blocks.at[number], blocks.at[number], send, block_recv.at[number], section, seq)
+
     def spread(number, slot):
-        for k, t in enumerate(others):
-            push(
-                blocks.at[number],
-                blocks.at[number],
-                plane_send.at[slot, k],
-                block_recv.at[number],
-                t,
-                j,
-            )
-        push(
-            blocks.at[number], blocks.at[number], twin_send.at[slot, 0], block_recv.at[number], s, twin
-        )
+        hand(number, plane_send.at[slot, 0], relayed, j)
+        hand(number, plane_send.at[slot, 1], direct, j)
+        hand(number, twin_send.at[slot, 0], s, twin)
 
     for k, i in enumerate(line):
         push(blocks.at[b], blocks.at[b], line_send.at[k], block_recv.at[b], s, i)
     spread(b, 0)
 
-    for k, t in enumerate(others):
-        arrived(wq.at[t, mine, :], w_recv.at[t])
-        push(wq.at[t, mine, :], wq.at[t, mine, :], wf_send.at[k], wf_recv.at[t], s, twin)
     theirs = pl.ds(pl.multiple_of((1 - c) * half, half), half)
     for k, t in enumerate(others):
         arrived(wq.at[t, theirs, :], wf_recv.at[t])
@@ -387,6 +393,11 @@
         number = i * n_section + s
         arrived(blocks.at[number], block_recv.at[number])
         spread(number, k + 1)
+    for i, seq in enumerate([j] + line):
+        number = seq * n_section + relayed
+        arrived(blocks.at[number], block_recv.at[number])
+        hand(number, plane_send.at[i, 2], direct, j)
+        hand(number, twin_send.at[i, 1], s, twin)
 
     for t in others:
         for h in range(n_section):
@@ -430,32 +441,32 @@
                 weights.astype(jnp.bfloat16), values, preferred_element_type=jnp.float32
             )
 
-    for i in range(n_line):
-        seq = ((z + i) % n_line) * 2 + c
-        for k, t in enumerate(others):
-            number = seq * n_section + t
-            arrived(blocks.at[number], block_recv.at[number])
-            push(
-                blocks.at[number],
-                blocks.at[number],
-                twin_send.at[i, k + 1],
-                block_recv.at[number],
-                s,
-                twin,
-            )
-        attend(seq)
-    for i in range(n_line):
+    def attend_twin(i):
         seq = ((z + i) % n_line) * 2 + (1 - c)
         for t in range(n_section):
             arrived(blocks.at[seq * n_section + t], block_recv.at[seq * n_section + t])
         attend(seq)
 
+    for i in range(n_line):
+        seq = ((z + i) % n_line) * 2 + c
+        for k, t in enumerate([direct, corner]):
+            number = seq * n_section + t
+            arrived(blocks.at[number], block_recv.at[number])
+            hand(number, twin_send.at[i, k + 2], s, twin)
+        attend(seq)
+        if i > 0:
+            attend_twin(i - 1)
+    attend_twin(n_line - 1)
+
     for h in range(n_section):
-        out_ref[s, :, h * head : (h + 1) * head] = (acc[h] / total[h]).astype(jnp.bfloat16)
-    for k, t in enumerate(others):
-        push(out_ref.at[s], out_ref.at[s], out_send.at[k], out_recv.at[s], t, j)
+        columns = pl.ds(h * head, head)
+        out_ref[s, :, columns] = (acc[h] / total[h]).astype(jnp.bfloat16)
+        piece = out_ref.at[s, :, columns]
+        for k, t in enumerate(others):
+            push(piece, piece, out_send.at[h, k], out_recv.at[s, h], t, j)
     for t in others:
-        arrived(out_ref.at[t], out_recv.at[t])
+        for h in range(n_section):
+            arrived(out_ref.at[t, :, pl.ds(h * head, head)], out_recv.at[t, h])
     for copy in pending:
         copy.wait_send()
 
@@ -476,19 +487,16 @@
     head = key_weight.shape[1]
     n_line = n_seq // 2
     n_blocks = n_section * n_seq
-    first = lax.axis_index("seq") * rows + lax.axis_index("section") * BLOCK
-    cosine, sine = tables(first + jnp.arange(BLOCK, dtype=jnp.int32), head)
-    sine = jnp.concatenate([-sine[:, : head // 2], sine[:, head // 2 :]], axis=1)
     vmem = pl.BlockSpec(memory_space=pltpu.VMEM)
     smem = pl.BlockSpec(memory_space=pltpu.SMEM)
-    anywhere = pl.BlockSpec(memory_space=pl.ANY)
+    anywhere = pl.BlockSpec(memory_space=pltpu.HBM)
     dma = pltpu.SemaphoreType.DMA
     bf16 = jnp.bfloat16
     f32 = jnp.float32
     attended = pl.pallas_call(
         functools.partial(fused, n_section, n_line),
         out_shape=jax.ShapeDtypeStruct((n_section, BLOCK, n_section * head), bf16),
-        in_specs=[anywhere, vmem, anywhere, anywhere, anywhere, vmem, vmem, smem, smem],
+        in_specs=[anywhere, vmem, anywhere, anywhere, anywhere, smem, smem],
         out_specs=vmem,
         scratch_shapes=[
             pltpu.VMEM((rows, width), bf16),
@@ -506,6 +514,7 @@
             pltpu.VMEM((n_section, BLOCK, head), f32),
             pltpu.VMEM((n_section, BLOCK, head), f32),
             dma((5,)),
+            dma((n_section,)),
             dma((n_section - 1,)),
             dma((n_section,)),
             dma((n_section - 1,)),
@@ -520,20 +529,18 @@
             dma((n_line, n_section - 1)),
             dma((n_line, n_section)),
             dma((n_blocks,)),
-            dma((n_section - 1,)),
-            dma((n_section,)),
+            dma((n_section, n_section - 1)),
+            dma((n_section, n_section)),
         ],
         compiler_params=pltpu.CompilerParams(
-            collective_id=0, has_side_effects=True, vmem_limit_bytes=40 * 1024 * 1024
+            collective_id=0, has_side_effects=True, vmem_limit_bytes=60 * 1024 * 1024
         ),
     )(
         hidden,
-        norm_gain.reshape(1, width),
+        norm_gain,
         query_weight,
         key_weight,
         value_weight,
-        cosine,
-        sine,
         block_reach,
         header_ids,
     )

time: 62.8 us -> 56.6 us (0.901)
  local copies, waits for them, and re-layouts: 6.43 us -> 0.01 us
  matrix products: 1.71 us -> 2.73 us
    unnamed x14 -> x2, local copies, waits for them, and re-layouts: 5.66 us -> 0.01 us
    dot_general x1, matrix products: 1.71 us -> 2.73 us  [on_device_fused(): jnp.dot(attended.reshape(rows, n_section * head), output_weight, preferre...]
    reshape x1 -> x0, local copies, waits for them, and re-layouts: 0.78 us -> none  [on_device_fused(): norm_gain.reshape(1, width)]
where the time goes in v2:
time: 56.6 us; the launch traced here: 56.4 us
  Pallas kernels  53.6 us (95%)
  matrix products  2.73 us (5%)
    pallas_call x1, Pallas kernels, on_device_fused(): pl.pallas_call(functools.partial(fused, n_section, n_line), out_shape=jax...  53.6 us
    dot_general x1, matrix products, on_device_fused(): jnp.dot(attended.reshape(rows, n_section * head), output_weight, preferre...  2.73 us

profile of v2, /device:TPU:0, one launch (start us, length us, event | category | flops | bytes accessed | tf_op | source)
XLA Modules:
  0.0 56.4 jit_solution(682664731880709046)
XLA Ops:
  0.0 0.0 copy-start
  0.0 53.6 %shard_map.82 = bf16[4,128,512]{2,1,0:T(8,128)(2,1)} custom-call(bf16[512,1024]{1,0:T(8,128)(2,1)} %hidden_ref.1, bf16[1024]{0:T(1024)(128)(2,1)} %gain_ref.1, bf16[4096,128]{1,0:T(8,128)(2,1)} %query_ref.1, bf16[1024,128]{1,0:T(8,128)(2,1)} %key_ref.1, bf16[1024,128]{1,0:T(8,128)(2,1)} %value_ref.1, s32[4]{0:T(128)} %reach_ref.1, s32[2]{0:T(128)} %ids_ref.1), custom_call_target="tpu_custom_call" | custom-call | tf_op jit(solution)/shard_map/pallas_call | solution.py:496
  53.7 0.0 copy-done
  53.7 2.7 %convolution_convert_fusion = bf16[512,1024]{1,0:T(8,128)(2,1)} fusion(bf16[512,512]{1,0:T(8,128)(2,1)} %bitcast.3, bf16[512,1024]{1,0:T(8,128)(2,1)S(1)} %copy-done), kind=kOutput, calls=%fused_computation | convolution fusion | flops 537395200 | bytes 2621440 | tf_op jit(solution)/shard_map/dot_general | solution.py:547
Async XLA Ops:
  0.0 53.7 %copy-start = (bf16[512,1024]{1,0:T(8,128)(2,1)S(1)}, bf16[512,1024]{1,0:T(8,128)(2,1)}, u32[]{:S(2)}) copy-start(bf16[512,1024]{1,0:T(8,128)(2,1)} %param.13) | copy-start | bytes 3145732

commit v3 on v2

--- a/solution.py
+++ b/solution.py
@@ -205,10 +205,11 @@
     ids_ref,
     out_ref,
     x,
-    normed,
+    scaled,
     wq,
     wkv,
     squares,
+    squares_got,
     kv_part,
     kv_got,
     q_part,
@@ -289,7 +290,22 @@
     friends = [(t, j) for t in others] + [(s, i) for i in line] + [(s, twin)]
     for friend in friends:
         pl.semaphore_signal(barrier, inc=1, device_id=friend, device_id_type=MESH)
+
+    gain = gain_ref[...].astype(jnp.float32).reshape(1, width)
+    for r in range(n_section):
+        get_x[r].wait()
+        part = x[r * BLOCK : (r + 1) * BLOCK, :].astype(jnp.float32)
+        scaled[r * BLOCK : (r + 1) * BLOCK, :] = (part * gain).astype(jnp.bfloat16)
+    get_k.wait()
+    get_v.wait()
+    kv_part[...] = (
+        jnp.dot(scaled[...], wkv[...], preferred_element_type=jnp.float32)
+        .astype(jnp.bfloat16)
+        .reshape(kv_part.shape)
+    )
     pl.semaphore_wait(barrier, len(friends))
+    for k, t in enumerate(others):
+        push(kv_part.at[t], kv_got.at[s], kv_send.at[k], kv_recv.at[s], t, j)
 
     mine = pl.ds(pl.multiple_of(c * half, half), half)
     for k, t in enumerate(others):
@@ -302,6 +318,13 @@
             j,
         )
 
+    for r in range(n_section):
+        part = x[r * BLOCK : (r + 1) * BLOCK, :].astype(jnp.float32)
+        column = jnp.sum(part * part, axis=1, keepdims=True)
+        squares[r] = jnp.transpose(jnp.broadcast_to(column, (BLOCK, BLOCK)))[:8, :]
+    for k, t in enumerate(others):
+        push(squares.at[t], squares_got.at[s], sq_send.at[k], sq_recv.at[s], t, j)
+
     b = j * n_section + s
     lanes = lax.broadcasted_iota(jnp.int32, (BLOCK, head), 1)
     positions = b * BLOCK + lax.broadcasted_iota(jnp.int32, (BLOCK, head), 0)
@@ -310,39 +333,10 @@
     cosine = jnp.cos(angles)
     sine = jnp.where(lanes < head // 2, -1.0, 1.0) * jnp.sin(angles)
 
-    for r in range(n_section):
-        get_x[r].wait()
-        part = x[r * BLOCK : (r + 1) * BLOCK, :].astype(jnp.float32)
-        column = jnp.sum(part * part, axis=1, keepdims=True)
-        squares[s, r] = jnp.transpose(jnp.broadcast_to(column, (BLOCK, BLOCK)))[:8, :]
-    for k, t in enumerate(others):
-        push(squares.at[s], squares.at[s], sq_send.at[k], sq_recv.at[s], t, j)
-    for t in others:
-        arrived(squares.at[t], sq_recv.at[t])
-    sums = squares[0]
-    for t in range(1, n_section):
-        sums = sums + squares[t]
-    scaling = lax.rsqrt(sums / (width * n_section) + EPSILON)
-    gain = gain_ref[...].astype(jnp.float32).reshape(1, width)
-    for r in range(n_section):
-        column = jnp.transpose(jnp.broadcast_to(scaling[r, 0:1, :], (BLOCK, BLOCK)))[:, 0:1]
-        part = x[r * BLOCK : (r + 1) * BLOCK, :].astype(jnp.float32)
-        normed[r * BLOCK : (r + 1) * BLOCK, :] = (part * column * gain).astype(jnp.bfloat16)
-
-    get_k.wait()
-    get_v.wait()
-    kv_part[...] = (
-        jnp.dot(normed[...], wkv[...], preferred_element_type=jnp.float32)
-        .astype(jnp.bfloat16)
-        .reshape(kv_part.shape)
-    )
-    for k, t in enumerate(others):
-        push(kv_part.at[t], kv_got.at[s], kv_send.at[k], kv_recv.at[s], t, j)
-
     def project(k):
         owner = (s + k) % n_section
         q_part[k] = (
-            jnp.dot(normed[...], wq[owner], preferred_element_type=jnp.float32)
+            jnp.dot(scaled[...], wq[owner], preferred_element_type=jnp.float32)
             .astype(jnp.bfloat16)
             .reshape(q_part.shape[1:])
         )
@@ -351,20 +345,24 @@
 
     get_q.wait()
     project(0)
-    for k, t in enumerate(others):
-        arrived(wq.at[t, mine, :], w_recv.at[t])
-        push(wq.at[t, mine, :], wq.at[t, mine, :], wf_send.at[k], wf_recv.at[t], s, twin)
 
     def turned(values):
         return values * cosine + pltpu.roll(values, head // 2, axis=1) * sine
 
+    for t in others:
+        arrived(squares_got.at[t], sq_recv.at[t])
+    sums = squares[s]
+    for t in others:
+        sums = sums + squares_got[t]
+    scaling = lax.rsqrt(sums / (width * n_section) + EPSILON)
+    scaling = jnp.transpose(jnp.broadcast_to(scaling[0:1, :], (BLOCK, BLOCK)))
     for t in others:
         arrived(kv_got.at[t], kv_recv.at[t])
     kv = kv_part[s].astype(jnp.float32)
     for t in others:
         kv = kv + kv_got[t].astype(jnp.float32)
-    blocks[b, :, 0:head] = turned(kv[:, :head]).astype(jnp.bfloat16)
-    blocks[b, :, head : 2 * head] = kv[:, head:].astype(jnp.bfloat16)
+    blocks[b, :, 0:head] = turned(kv[:, :head] * scaling).astype(jnp.bfloat16)
+    blocks[b, :, head : 2 * head] = (kv[:, head:] * scaling).astype(jnp.bfloat16)
 
     across = s + 1 - 2 * (s % 2)
     along = (s + 2) % n_section
@@ -384,20 +382,26 @@
         push(blocks.at[b], blocks.at[b], line_send.at[k], block_recv.at[b], s, i)
     spread(b, 0)
 
+    def relay(i, seq):
+        number = seq * n_section + relayed
+        arrived(blocks.at[number], block_recv.at[number])
+        hand(number, plane_send.at[i, 2], direct, j)
+        hand(number, twin_send.at[i, 1], s, twin)
+
+    for k, i in enumerate(line):
+        number = i * n_section + s
+        arrived(blocks.at[number], block_recv.at[number])
+        spread(number, k + 1)
+    for k, t in enumerate(others):
+        arrived(wq.at[t, mine, :], w_recv.at[t])
+        push(wq.at[t, mine, :], wq.at[t, mine, :], wf_send.at[k], wf_recv.at[t], s, twin)
+    relay(0, j)
     theirs = pl.ds(pl.multiple_of((1 - c) * half, half), half)
     for k, t in enumerate(others):
         arrived(wq.at[t, theirs, :], wf_recv.at[t])
         project(k + 1)
-
     for k, i in enumerate(line):
-        number = i * n_section + s
-        arrived(blocks.at[number], block_recv.at[number])
-        spread(number, k + 1)
-    for i, seq in enumerate([j] + line):
-        number = seq * n_section + relayed
-        arrived(blocks.at[number], block_recv.at[number])
-        hand(number, plane_send.at[i, 2], direct, j)
-        hand(number, twin_send.at[i, 1], s, twin)
+        relay(k + 1, i)
 
     for t in others:
         for h in range(n_section):
@@ -407,7 +411,7 @@
         value = q_part[place, s].astype(jnp.float32)
         for t in others:
             value = value + q_got[t, h].astype(jnp.float32)
-        queries[h] = turned(value).astype(jnp.bfloat16)
+        queries[h] = turned(value * scaling).astype(jnp.bfloat16)
 
     first = ids_ref[0]
     second = ids_ref[1]
@@ -503,7 +507,8 @@
             pltpu.VMEM((rows, width), bf16),
             pltpu.VMEM((n_section, width, head), bf16),
             pltpu.VMEM((width, 2 * head), bf16),
-            pltpu.VMEM((n_section, n_section, 8, BLOCK), f32),
+            pltpu.VMEM((n_section, 8, BLOCK), f32),
+            pltpu.VMEM((n_section, 8, BLOCK), f32),
             pltpu.VMEM((n_section, BLOCK, 2 * head), bf16),
             pltpu.VMEM((n_section, BLOCK, 2 * head), bf16),
             pltpu.VMEM((n_section, n_section, BLOCK, head), bf16),

time: 56.6 us -> 56.8 us (level)
  no operation moved by 1% of the time
where the time goes in v3:
time: 56.8 us; the launch traced here: 56.6 us
  Pallas kernels  53.9 us (95%)
  matrix products  2.73 us (5%)
    pallas_call x1, Pallas kernels, on_device_fused(): pl.pallas_call(functools.partial(fused, n_section, n_line), out_shape=jax...  53.9 us
    dot_general x1, matrix products, on_device_fused(): jnp.dot(attended.reshape(rows, n_section * head), output_weight, preferre...  2.73 us

profile of v3, /device:TPU:0, one launch (start us, length us, event | category | flops | bytes accessed | tf_op | source)
XLA Modules:
  0.0 56.6 jit_solution(113959564318460999)
XLA Ops:
  0.0 0.0 copy-start
  0.0 53.9 %shard_map.82 = bf16[4,128,512]{2,1,0:T(8,128)(2,1)} custom-call(bf16[512,1024]{1,0:T(8,128)(2,1)} %hidden_ref.1, bf16[1024]{0:T(1024)(128)(2,1)} %gain_ref.1, bf16[4096,128]{1,0:T(8,128)(2,1)} %query_ref.1, bf16[1024,128]{1,0:T(8,128)(2,1)} %key_ref.1, bf16[1024,128]{1,0:T(8,128)(2,1)} %value_ref.1, s32[4]{0:T(128)} %reach_ref.1, s32[2]{0:T(128)} %ids_ref.1), custom_call_target="tpu_custom_call" | custom-call | tf_op jit(solution)/shard_map/pallas_call | solution.py:500
  53.9 0.0 copy-done
  53.9 2.7 %convolution_convert_fusion = bf16[512,1024]{1,0:T(8,128)(2,1)} fusion(bf16[512,512]{1,0:T(8,128)(2,1)} %bitcast.3, bf16[512,1024]{1,0:T(8,128)(2,1)S(1)} %copy-done), kind=kOutput, calls=%fused_computation | convolution fusion | flops 537395200 | bytes 2621440 | tf_op jit(solution)/shard_map/dot_general | solution.py:552
Async XLA Ops:
  0.0 53.9 %copy-start = (bf16[512,1024]{1,0:T(8,128)(2,1)S(1)}, bf16[512,1024]{1,0:T(8,128)(2,1)}, u32[]{:S(2)}) copy-start(bf16[512,1024]{1,0:T(8,128)(2,1)} %param.13) | copy-start | bytes 3145732

commit v4 on v3

--- a/solution.py
+++ b/solution.py
@@ -217,12 +217,16 @@
     blocks,
     queries,
     top,
-    total,
+    fade,
     acc,
+    scores,
+    weights,
     local_sem,
     x_sem,
     w_send,
     w_recv,
+    wz_send,
+    wz_recv,
     wf_send,
     wf_recv,
     sq_send,
@@ -307,11 +311,20 @@
     for k, t in enumerate(others):
         push(kv_part.at[t], kv_got.at[s], kv_send.at[k], kv_recv.at[s], t, j)
 
+    quarter = half // 2
+    partner = (z + 1 - 2 * (z % 2)) * 2 + c
     mine = pl.ds(pl.multiple_of(c * half, half), half)
+    near = pl.ds(pl.multiple_of(c * half + (z % 2) * quarter, quarter), quarter)
+    far = pl.ds(pl.multiple_of(c * half + (1 - z % 2) * quarter, quarter), quarter)
     for k, t in enumerate(others):
         push(
-            query_ref.at[pl.ds(pl.multiple_of(t * width + c * half, half), half), :],
-            wq.at[s, mine, :],
+            query_ref.at[
+                pl.ds(
+                    pl.multiple_of(t * width + c * half + (z % 2) * quarter, quarter), quarter
+                ),
+                :,
+            ],
+            wq.at[s, near, :],
             w_send.at[k],
             w_recv.at[s],
             t,
@@ -361,7 +374,7 @@
     kv = kv_part[s].astype(jnp.float32)
     for t in others:
         kv = kv + kv_got[t].astype(jnp.float32)
-    blocks[b, :, 0:head] = turned(kv[:, :head] * scaling).astype(jnp.bfloat16)
+    blocks[b, :, 0:head] = jnp.transpose(turned(kv[:, :head] * scaling)).astype(jnp.bfloat16)
     blocks[b, :, head : 2 * head] = (kv[:, head:] * scaling).astype(jnp.bfloat16)
 
     across = s + 1 - 2 * (s % 2)
@@ -388,12 +401,15 @@
         hand(number, plane_send.at[i, 2], direct, j)
         hand(number, twin_send.at[i, 1], s, twin)
 
+    for k, t in enumerate(others):
+        arrived(wq.at[t, near, :], w_recv.at[t])
+        push(wq.at[t, near, :], wq.at[t, near, :], wz_send.at[k], wz_recv.at[t], s, partner)
     for k, i in enumerate(line):
         number = i * n_section + s
         arrived(blocks.at[number], block_recv.at[number])
         spread(number, k + 1)
     for k, t in enumerate(others):
-        arrived(wq.at[t, mine, :], w_recv.at[t])
+        arrived(wq.at[t, far, :], wz_recv.at[t])
         push(wq.at[t, mine, :], wq.at[t, mine, :], wf_send.at[k], wf_recv.at[t], s, twin)
     relay(0, j)
     theirs = pl.ds(pl.multiple_of((1 - c) * half, half), half)
@@ -411,60 +427,67 @@
         value = q_part[place, s].astype(jnp.float32)
         for t in others:
             value = value + q_got[t, h].astype(jnp.float32)
-        queries[h] = turned(value * scaling).astype(jnp.bfloat16)
+        queries[h * BLOCK : (h + 1) * BLOCK, :] = turned(value * scaling).astype(jnp.bfloat16)
 
     first = ids_ref[0]
     second = ids_ref[1]
     own_header = jnp.logical_or(first == b, second == b)
     limit = jnp.where(own_header, n_section * n_line * 2, reach_ref[s])
-    group = n_section * BLOCK
+    group = 2 * n_section
+    keys_wide = group * BLOCK
     factor = 1.4426950408889634 / math.sqrt(head)
     top[...] = jnp.full(top.shape, LOW, jnp.float32)
-    total[...] = jnp.zeros(total.shape, jnp.float32)
     acc[...] = jnp.zeros(acc.shape, jnp.float32)
-
-    def attend(seq):
-        start = seq * n_section
-        numbers = start + lax.broadcasted_iota(jnp.int32, (1, group), 1) // BLOCK
+    ones = jnp.ones((keys_wide, head), jnp.bfloat16)
+    strip = 32
+
+    def attend(place):
+        start = place * group
+        numbers = start + lax.broadcasted_iota(jnp.int32, (1, keys_wide), 1) // BLOCK
         valid = (numbers == first) | (numbers == second) | (jnp.abs(numbers - b) <= limit)
         bias = jnp.where(valid, 0.0, LOW)
-        keys = blocks[pl.ds(start, n_section), :, 0:head].reshape(group, head)
-        values = blocks[pl.ds(start, n_section), :, head : 2 * head].reshape(group, head)
-        for h in range(n_section):
-            scores = lax.dot_general(
-                queries[h], keys, (((1,), (1,)), ((), ())), preferred_element_type=jnp.float32
-            )
-            scores = scores * factor + bias
-            before = top[h]
-            after = jnp.maximum(before, jnp.max(scores, axis=1, keepdims=True))
-            fade = jnp.exp2(before - after)
-            weights = jnp.exp2(scores - after[:, 0:1])
-            top[h] = after
-            total[h] = total[h] * fade + jnp.sum(weights, axis=1, keepdims=True)
-            acc[h] = acc[h] * fade + jnp.dot(
-                weights.astype(jnp.bfloat16), values, preferred_element_type=jnp.float32
-            )
-
-    def attend_twin(i):
-        seq = ((z + i) % n_line) * 2 + (1 - c)
-        for t in range(n_section):
-            arrived(blocks.at[seq * n_section + t], block_recv.at[seq * n_section + t])
-        attend(seq)
-
-    for i in range(n_line):
+        keys = jnp.concatenate([blocks[start + n, :, 0:head] for n in range(group)], axis=1)
+        scores[...] = jnp.dot(queries[...], keys, preferred_element_type=jnp.float32)
+        for r in range(0, n_section * BLOCK, strip):
+            rows = pl.ds(r, strip)
+            part = scores[rows, :] * factor + bias
+            before = top[rows, :]
+            after = jnp.maximum(before, jnp.max(part, axis=1, keepdims=True))
+            weights[rows, :] = jnp.exp2(part - after[:, 0:1]).astype(jnp.bfloat16)
+            fade[rows, :] = jnp.exp2(before - after)
+            top[rows, :] = after
+        values = blocks[pl.ds(start, group), :, head : 2 * head].reshape(keys_wide, head)
+        gained = jnp.dot(
+            weights[...],
+            jnp.concatenate([values, ones], axis=1),
+            preferred_element_type=jnp.float32,
+        )
+        factors = fade[...]
+        acc[:, 0:head] = acc[:, 0:head] * factors + gained[:, 0:head]
+        acc[:, head : 2 * head] = acc[:, head : 2 * head] * factors + gained[:, head : 2 * head]
+
+    def pass_on(i):
         seq = ((z + i) % n_line) * 2 + c
         for k, t in enumerate([direct, corner]):
             number = seq * n_section + t
             arrived(blocks.at[number], block_recv.at[number])
             hand(number, twin_send.at[i, k + 2], s, twin)
-        attend(seq)
-        if i > 0:
-            attend_twin(i - 1)
-    attend_twin(n_line - 1)
+
+    pass_on(0)
+    for i in range(n_line):
+        if i + 1 < n_line:
+            pass_on(i + 1)
+        place = (z + i) % n_line
+        for t in range(n_section):
+            number = (place * 2 + 1 - c) * n_section + t
+            arrived(blocks.at[number], block_recv.at[number])
+        attend(place)
 
     for h in range(n_section):
         columns = pl.ds(h * head, head)
-        out_ref[s, :, columns] = (acc[h] / total[h]).astype(jnp.bfloat16)
+        out_ref[s, :, columns] = (
+            acc[h * BLOCK : (h + 1) * BLOCK, 0:head] / acc[h * BLOCK : (h + 1) * BLOCK, head : 2 * head]
+        ).astype(jnp.bfloat16)
         piece = out_ref.at[s, :, columns]
         for k, t in enumerate(others):
             push(piece, piece, out_send.at[h, k], out_recv.at[s, h], t, j)
@@ -514,11 +537,15 @@
             pltpu.VMEM((n_section, n_section, BLOCK, head), bf16),
             pltpu.VMEM((n_section, n_section, BLOCK, head), bf16),
             pltpu.VMEM((n_blocks, BLOCK, 2 * head), bf16),
-            pltpu.VMEM((n_section, BLOCK, head), bf16),
-            pltpu.VMEM((n_section, BLOCK, head), f32),
-            pltpu.VMEM((n_section, BLOCK, head), f32),
-            pltpu.VMEM((n_section, BLOCK, head), f32),
+            pltpu.VMEM((n_section * BLOCK, head), bf16),
+            pltpu.VMEM((n_section * BLOCK, head), f32),
+            pltpu.VMEM((n_section * BLOCK, head), f32),
+            pltpu.VMEM((n_section * BLOCK, 2 * head), f32),
+            pltpu.VMEM((n_section * BLOCK, 2 * n_section * BLOCK), f32),
+            pltpu.VMEM((n_section * BLOCK, 2 * n_section * BLOCK), bf16),
             dma((5,)),
+            dma((n_section,)),
+            dma((n_section - 1,)),
             dma((n_section,)),
             dma((n_section - 1,)),
             dma((n_section,)),

time: 56.8 us -> 51.9 us (0.914)
  Pallas kernels: 53.9 us -> 49 us
    pallas_call x1, Pallas kernels: 53.9 us -> 49 us  [on_device_fused(): pl.pallas_call(functools.partial(fused, n_section, n_line), out_shape=jax...]
where the time goes in v4:
time: 51.9 us; the launch traced here: 51.7 us
  Pallas kernels  49 us (94%)
  matrix products  2.73 us (5%)
    pallas_call x1, Pallas kernels, on_device_fused(): pl.pallas_call(functools.partial(fused, n_section, n_line), out_shape=jax...  49 us
    dot_general x1, matrix products, on_device_fused(): jnp.dot(attended.reshape(rows, n_section * head), output_weight, preferre...  2.73 us

profile of v4, /device:TPU:0, one launch (start us, length us, event | category | flops | bytes accessed | tf_op | source)
XLA Modules:
  0.0 51.7 jit_solution(18129766558514162157)
XLA Ops:
  0.0 0.0 copy-start
  0.0 49.0 %shard_map.82 = bf16[4,128,512]{2,1,0:T(8,128)(2,1)} custom-call(bf16[512,1024]{1,0:T(8,128)(2,1)} %hidden_ref.1, bf16[1024]{0:T(1024)(128)(2,1)} %gain_ref.1, bf16[4096,128]{1,0:T(8,128)(2,1)} %query_ref.1, bf16[1024,128]{1,0:T(8,128)(2,1)} %key_ref.1, bf16[1024,128]{1,0:T(8,128)(2,1)} %value_ref.1, s32[4]{0:T(128)} %reach_ref.1, s32[2]{0:T(128)} %ids_ref.1), custom_call_target="tpu_custom_call" | custom-call | tf_op jit(solution)/shard_map/pallas_call | solution.py:523
  49.0 0.0 copy-done
  49.0 2.7 %convolution_convert_fusion = bf16[512,1024]{1,0:T(8,128)(2,1)} fusion(bf16[512,512]{1,0:T(8,128)(2,1)} %bitcast.3, bf16[512,1024]{1,0:T(8,128)(2,1)S(1)} %copy-done), kind=kOutput, calls=%fused_computation | convolution fusion | flops 537395200 | bytes 2621440 | tf_op jit(solution)/shard_map/dot_general | solution.py:579
Async XLA Ops:
  0.0 49.0 %copy-start = (bf16[512,1024]{1,0:T(8,128)(2,1)S(1)}, bf16[512,1024]{1,0:T(8,128)(2,1)}, u32[]{:S(2)}) copy-start(bf16[512,1024]{1,0:T(8,128)(2,1)} %param.13) | copy-start | bytes 3145732

commit v5 on v4

--- a/solution.py
+++ b/solution.py
@@ -214,7 +214,8 @@
     kv_got,
     q_part,
     q_got,
-    blocks,
+    key_blocks,
+    value_blocks,
     queries,
     top,
     fade,
@@ -238,7 +239,11 @@
     line_send,
     plane_send,
     twin_send,
-    block_recv,
+    key_recv,
+    value_plane_send,
+    value_line_send,
+    value_twin_send,
+    value_recv,
     out_send,
     out_recv,
 ):
@@ -295,21 +300,7 @@
     for friend in friends:
         pl.semaphore_signal(barrier, inc=1, device_id=friend, device_id_type=MESH)
 
-    gain = gain_ref[...].astype(jnp.float32).reshape(1, width)
-    for r in range(n_section):
-        get_x[r].wait()
-        part = x[r * BLOCK : (r + 1) * BLOCK, :].astype(jnp.float32)
-        scaled[r * BLOCK : (r + 1) * BLOCK, :] = (part * gain).astype(jnp.bfloat16)
-    get_k.wait()
-    get_v.wait()
-    kv_part[...] = (
-        jnp.dot(scaled[...], wkv[...], preferred_element_type=jnp.float32)
-        .astype(jnp.bfloat16)
-        .reshape(kv_part.shape)
-    )
     pl.semaphore_wait(barrier, len(friends))
-    for k, t in enumerate(others):
-        push(kv_part.at[t], kv_got.at[s], kv_send.at[k], kv_recv.at[s], t, j)
 
     quarter = half // 2
     partner = (z + 1 - 2 * (z % 2)) * 2 + c
@@ -331,6 +322,21 @@
             j,
         )
 
+    gain = gain_ref[...].astype(jnp.float32).reshape(1, width)
+    for r in range(n_section):
+        get_x[r].wait()
+        part = x[r * BLOCK : (r + 1) * BLOCK, :].astype(jnp.float32)
+        scaled[r * BLOCK : (r + 1) * BLOCK, :] = (part * gain).astype(jnp.bfloat16)
+    get_k.wait()
+    get_v.wait()
+    kv_part[...] = (
+        jnp.dot(scaled[...], wkv[...], preferred_element_type=jnp.float32)
+        .astype(jnp.bfloat16)
+        .reshape(kv_part.shape)
+    )
+    for k, t in enumerate(others):
+        push(kv_part.at[t], kv_got.at[s], kv_send.at[k], kv_recv.at[s], t, j)
+
     for r in range(n_section):
         part = x[r * BLOCK : (r + 1) * BLOCK, :].astype(jnp.float32)
         column = jnp.sum(part * part, axis=1, keepdims=True)
@@ -358,6 +364,9 @@
 
     get_q.wait()
     project(0)
+    for k, t in enumerate(others):
+        arrived(wq.at[t, near, :], w_recv.at[t])
+        push(wq.at[t, near, :], wq.at[t, near, :], wz_send.at[k], wz_recv.at[t], s, partner)
 
     def turned(values):
         return values * cosine + pltpu.roll(values, head // 2, axis=1) * sine
@@ -374,8 +383,8 @@
     kv = kv_part[s].astype(jnp.float32)
     for t in others:
         kv = kv + kv_got[t].astype(jnp.float32)
-    blocks[b, :, 0:head] = jnp.transpose(turned(kv[:, :head] * scaling)).astype(jnp.bfloat16)
-    blocks[b, :, head : 2 * head] = (kv[:, head:] * scaling).astype(jnp.bfloat16)
+    key_blocks[b] = jnp.transpose(turned(kv[:, :head] * scaling)).astype(jnp.bfloat16)
+    value_blocks[b] = (kv[:, head:] * scaling).astype(jnp.bfloat16)
 
     across = s + 1 - 2 * (s % 2)
     along = (s + 2) % n_section
@@ -383,41 +392,67 @@
     relayed = jnp.where(c == 0, across, along)
     direct = jnp.where(c == 0, along, across)
 
-    def hand(number, send, section, seq):
-        push(blocks.at[number], blocks.at[number], send, block_recv.at[number], section, seq)
-
-    def spread(number, slot):
-        hand(number, plane_send.at[slot, 0], relayed, j)
-        hand(number, plane_send.at[slot, 1], direct, j)
-        hand(number, twin_send.at[slot, 0], s, twin)
+    def hand_key(number, send, section, seq):
+        piece = key_blocks.at[number]
+        push(piece, piece, send, key_recv.at[number], section, seq)
+
+    def hand_value(number, send, section, seq):
+        piece = value_blocks.at[number]
+        push(piece, piece, send, value_recv.at[number], section, seq)
+
+    def await_key(number):
+        arrived(key_blocks.at[number], key_recv.at[number])
+
+    def await_value(number):
+        arrived(value_blocks.at[number], value_recv.at[number])
+
+    def spread_key(number, slot):
+        hand_key(number, plane_send.at[slot, 0], relayed, j)
+        hand_key(number, plane_send.at[slot, 1], direct, j)
+        hand_key(number, twin_send.at[slot, 0], s, twin)
+
+    def relay_key(slot, seq):
+        number = seq * n_section + relayed
+        await_key(number)
+        hand_key(number, plane_send.at[slot, 2], direct, j)
+        hand_key(number, twin_send.at[slot, 1], s, twin)
+
+    def spread_value(number, slot):
+        hand_value(number, value_twin_send.at[0, slot], s, twin)
+        for k, i in enumerate(line):
+            hand_value(number, value_line_send.at[slot, k], s, i)
 
     for k, i in enumerate(line):
-        push(blocks.at[b], blocks.at[b], line_send.at[k], block_recv.at[b], s, i)
-    spread(b, 0)
-
-    def relay(i, seq):
-        number = seq * n_section + relayed
-        arrived(blocks.at[number], block_recv.at[number])
-        hand(number, plane_send.at[i, 2], direct, j)
-        hand(number, twin_send.at[i, 1], s, twin)
-
-    for k, t in enumerate(others):
-        arrived(wq.at[t, near, :], w_recv.at[t])
-        push(wq.at[t, near, :], wq.at[t, near, :], wz_send.at[k], wz_recv.at[t], s, partner)
-    for k, i in enumerate(line):
-        number = i * n_section + s
-        arrived(blocks.at[number], block_recv.at[number])
-        spread(number, k + 1)
+        hand_key(b, line_send.at[k], s, i)
+    hand_value(b, value_plane_send.at[0], relayed, j)
+    hand_value(b, value_plane_send.at[1], direct, j)
+    spread_key(b, 0)
+    spread_value(b, 0)
+
+    number = j * n_section + relayed
+    await_value(number)
+    hand_value(number, value_plane_send.at[2], direct, j)
+    spread_value(number, 1)
     for k, t in enumerate(others):
         arrived(wq.at[t, far, :], wz_recv.at[t])
         push(wq.at[t, mine, :], wq.at[t, mine, :], wf_send.at[k], wf_recv.at[t], s, twin)
-    relay(0, j)
+    for k, i in enumerate(line):
+        number = i * n_section + s
+        await_key(number)
+        spread_key(number, k + 1)
+    number = j * n_section + direct
+    await_value(number)
+    spread_value(number, 2)
     theirs = pl.ds(pl.multiple_of((1 - c) * half, half), half)
     for k, t in enumerate(others):
         arrived(wq.at[t, theirs, :], wf_recv.at[t])
         project(k + 1)
+    relay_key(0, j)
+    number = j * n_section + corner
+    await_value(number)
+    spread_value(number, 3)
     for k, i in enumerate(line):
-        relay(k + 1, i)
+        relay_key(k + 1, i)
 
     for t in others:
         for h in range(n_section):
@@ -446,7 +481,7 @@
         numbers = start + lax.broadcasted_iota(jnp.int32, (1, keys_wide), 1) // BLOCK
         valid = (numbers == first) | (numbers == second) | (jnp.abs(numbers - b) <= limit)
         bias = jnp.where(valid, 0.0, LOW)
-        keys = jnp.concatenate([blocks[start + n, :, 0:head] for n in range(group)], axis=1)
+        keys = jnp.concatenate([key_blocks[start + n] for n in range(group)], axis=1)
         scores[...] = jnp.dot(queries[...], keys, preferred_element_type=jnp.float32)
         for r in range(0, n_section * BLOCK, strip):
             rows = pl.ds(r, strip)
@@ -456,7 +491,7 @@
             weights[rows, :] = jnp.exp2(part - after[:, 0:1]).astype(jnp.bfloat16)
             fade[rows, :] = jnp.exp2(before - after)
             top[rows, :] = after
-        values = blocks[pl.ds(start, group), :, head : 2 * head].reshape(keys_wide, head)
+        values = value_blocks[pl.ds(start, group)].reshape(keys_wide, head)
         gained = jnp.dot(
             weights[...],
             jnp.concatenate([values, ones], axis=1),
@@ -470,8 +505,13 @@
         seq = ((z + i) % n_line) * 2 + c
         for k, t in enumerate([direct, corner]):
             number = seq * n_section + t
-            arrived(blocks.at[number], block_recv.at[number])
-            hand(number, twin_send.at[i, k + 2], s, twin)
+            await_key(number)
+            hand_key(number, twin_send.at[i, k + 2], s, twin)
+        if i > 0:
+            for t in range(n_section):
+                number = seq * n_section + t
+                await_value(number)
+                hand_value(number, value_twin_send.at[i, t], s, twin)
 
     pass_on(0)
     for i in range(n_line):
@@ -480,7 +520,8 @@
         place = (z + i) % n_line
         for t in range(n_section):
             number = (place * 2 + 1 - c) * n_section + t
-            arrived(blocks.at[number], block_recv.at[number])
+            await_key(number)
+            await_value(number)
         attend(place)
 
     for h in range(n_section):
@@ -536,7 +577,8 @@
             pltpu.VMEM((n_section, BLOCK, 2 * head), bf16),
             pltpu.VMEM((n_section, n_section, BLOCK, head), bf16),
             pltpu.VMEM((n_section, n_section, BLOCK, head), bf16),
-            pltpu.VMEM((n_blocks, BLOCK, 2 * head), bf16),
+            pltpu.VMEM((n_blocks, head, BLOCK), bf16),
+            pltpu.VMEM((n_blocks, BLOCK, head), bf16),
             pltpu.VMEM((n_section * BLOCK, head), bf16),
             pltpu.VMEM((n_section * BLOCK, head), f32),
             pltpu.VMEM((n_section * BLOCK, head), f32),
@@ -561,6 +603,10 @@
             dma((n_line, n_section - 1)),
             dma((n_line, n_section)),
             dma((n_blocks,)),
+            dma((n_section - 1,)),
+            dma((n_section, n_line - 1)),
+            dma((n_line, n_section)),
+            dma((n_blocks,)),
             dma((n_section, n_section - 1)),
             dma((n_section, n_section)),
         ],

time: 51.9 us -> 51.4 us (level)
  Pallas kernels: 49 us -> 48.4 us
    pallas_call x1, Pallas kernels: 49 us -> 48.4 us  [on_device_fused(): pl.pallas_call(functools.partial(fused, n_section, n_line), out_shape=jax...]
where the time goes in v5:
time: 51.4 us; the launch traced here: 51.2 us
  Pallas kernels  48.4 us (94%)
  matrix products  2.73 us (5%)
    pallas_call x1, Pallas kernels, on_device_fused(): pl.pallas_call(functools.partial(fused, n_section, n_line), out_shape=jax...  48.4 us
    dot_general x1, matrix products, on_device_fused(): jnp.dot(attended.reshape(rows, n_section * head), output_weight, preferre...  2.73 us

profile of v5, /device:TPU:0, one launch (start us, length us, event | category | flops | bytes accessed | tf_op | source)
XLA Modules:
  0.0 51.2 jit_solution(16909026782798001526)
XLA Ops:
  0.0 0.0 copy-start
  0.0 48.4 %shard_map.82 = bf16[4,128,512]{2,1,0:T(8,128)(2,1)} custom-call(bf16[512,1024]{1,0:T(8,128)(2,1)} %hidden_ref.1, bf16[1024]{0:T(1024)(128)(2,1)} %gain_ref.1, bf16[4096,128]{1,0:T(8,128)(2,1)} %query_ref.1, bf16[1024,128]{1,0:T(8,128)(2,1)} %key_ref.1, bf16[1024,128]{1,0:T(8,128)(2,1)} %value_ref.1, s32[4]{0:T(128)} %reach_ref.1, s32[2]{0:T(128)} %ids_ref.1), custom_call_target="tpu_custom_call" | custom-call | tf_op jit(solution)/shard_map/pallas_call | solution.py:564
  48.5 0.0 copy-done
  48.5 2.7 %convolution_convert_fusion = bf16[512,1024]{1,0:T(8,128)(2,1)} fusion(bf16[512,512]{1,0:T(8,128)(2,1)} %bitcast.3, bf16[512,1024]{1,0:T(8,128)(2,1)S(1)} %copy-done), kind=kOutput, calls=%fused_computation | convolution fusion | flops 537395200 | bytes 2621440 | tf_op jit(solution)/shard_map/dot_general | solution.py:625
Async XLA Ops:
  0.0 48.5 %copy-start = (bf16[512,1024]{1,0:T(8,128)(2,1)S(1)}, bf16[512,1024]{1,0:T(8,128)(2,1)}, u32[]{:S(2)}) copy-start(bf16[512,1024]{1,0:T(8,128)(2,1)} %param.13) | copy-start | bytes 3145732

commit v6 on v5

--- a/solution.py
+++ b/solution.py
@@ -201,6 +201,7 @@
     query_ref,
     key_ref,
     value_ref,
+    project_ref,
     reach_ref,
     ids_ref,
     out_ref,
@@ -222,6 +223,9 @@
     acc,
     scores,
     weights,
+    attended,
+    wo,
+    result,
     local_sem,
     x_sem,
     w_send,
@@ -240,12 +244,16 @@
     plane_send,
     twin_send,
     key_recv,
+    key_twin_recv,
     value_plane_send,
     value_line_send,
     value_twin_send,
     value_recv,
+    value_line_recv,
+    value_twin_recv,
     out_send,
     out_recv,
+    store_sem,
 ):
     width = x.shape[1]
     half = width // 2
@@ -291,9 +299,11 @@
     get_q = pltpu.make_async_copy(
         query_ref.at[pl.ds(pl.multiple_of(s * width, width), width), :], wq.at[s], local_sem.at[3]
     )
+    get_o = pltpu.make_async_copy(project_ref, wo, local_sem.at[0])
     get_k.start()
     get_v.start()
     get_q.start()
+    get_o.start()
 
     barrier = pltpu.get_barrier_semaphore()
     friends = [(t, j) for t in others] + [(s, i) for i in line] + [(s, twin)]
@@ -354,16 +364,16 @@
 
     def project(k):
         owner = (s + k) % n_section
-        q_part[k] = (
+        q_part[:, k] = (
             jnp.dot(scaled[...], wq[owner], preferred_element_type=jnp.float32)
             .astype(jnp.bfloat16)
-            .reshape(q_part.shape[1:])
+            .reshape(n_section, BLOCK, head)
         )
-        for i, t in enumerate(others):
-            push(q_part.at[k, t], q_got.at[s, owner], q_send.at[k, i], q_recv.at[s, owner], t, j)
 
     get_q.wait()
     project(0)
+    for k, t in enumerate(others):
+        push(q_part.at[t, 0], q_got.at[s, 0], q_send.at[0, k], q_recv.at[s, 0], t, j)
     for k, t in enumerate(others):
         arrived(wq.at[t, near, :], w_recv.at[t])
         push(wq.at[t, near, :], wq.at[t, near, :], wz_send.at[k], wz_recv.at[t], s, partner)
@@ -396,43 +406,37 @@
         piece = key_blocks.at[number]
         push(piece, piece, send, key_recv.at[number], section, seq)
 
-    def hand_value(number, send, section, seq):
+    def hand_value(number, send, section):
         piece = value_blocks.at[number]
-        push(piece, piece, send, value_recv.at[number], section, seq)
+        push(piece, piece, send, value_recv.at[number - j * n_section], section, j)
 
     def await_key(number):
         arrived(key_blocks.at[number], key_recv.at[number])
 
     def await_value(number):
-        arrived(value_blocks.at[number], value_recv.at[number])
+        arrived(value_blocks.at[number], value_recv.at[number - j * n_section])
+
+    def plane(blocks, seq):
+        return blocks.at[pl.ds(seq * n_section, n_section)]
 
     def spread_key(number, slot):
         hand_key(number, plane_send.at[slot, 0], relayed, j)
         hand_key(number, plane_send.at[slot, 1], direct, j)
-        hand_key(number, twin_send.at[slot, 0], s, twin)
 
     def relay_key(slot, seq):
         number = seq * n_section + relayed
         await_key(number)
         hand_key(number, plane_send.at[slot, 2], direct, j)
-        hand_key(number, twin_send.at[slot, 1], s, twin)
-
-    def spread_value(number, slot):
-        hand_value(number, value_twin_send.at[0, slot], s, twin)
-        for k, i in enumerate(line):
-            hand_value(number, value_line_send.at[slot, k], s, i)
 
     for k, i in enumerate(line):
         hand_key(b, line_send.at[k], s, i)
-    hand_value(b, value_plane_send.at[0], relayed, j)
-    hand_value(b, value_plane_send.at[1], direct, j)
+    hand_value(b, value_plane_send.at[0], relayed)
+    hand_value(b, value_plane_send.at[1], direct)
     spread_key(b, 0)
-    spread_value(b, 0)
 
     number = j * n_section + relayed
     await_value(number)
-    hand_value(number, value_plane_send.at[2], direct, j)
-    spread_value(number, 1)
+    hand_value(number, value_plane_send.at[2], direct)
     for k, t in enumerate(others):
         arrived(wq.at[t, far, :], wz_recv.at[t])
         push(wq.at[t, mine, :], wq.at[t, mine, :], wf_send.at[k], wf_recv.at[t], s, twin)
@@ -440,28 +444,31 @@
         number = i * n_section + s
         await_key(number)
         spread_key(number, k + 1)
-    number = j * n_section + direct
-    await_value(number)
-    spread_value(number, 2)
+    await_value(j * n_section + direct)
+    await_value(j * n_section + corner)
+    whole = plane(value_blocks, j)
+    for k, i in enumerate(line):
+        push(whole, whole, value_line_send.at[k], value_line_recv.at[z], s, i)
+    push(whole, whole, value_twin_send.at[0], value_twin_recv.at[z], s, twin)
     theirs = pl.ds(pl.multiple_of((1 - c) * half, half), half)
     for k, t in enumerate(others):
         arrived(wq.at[t, theirs, :], wf_recv.at[t])
         project(k + 1)
+    rest = pl.ds(1, n_section - 1)
+    for k, t in enumerate(others):
+        push(q_part.at[t, rest], q_got.at[s, rest], q_send.at[1, k], q_recv.at[s, 1], t, j)
     relay_key(0, j)
-    number = j * n_section + corner
-    await_value(number)
-    spread_value(number, 3)
     for k, i in enumerate(line):
         relay_key(k + 1, i)
 
     for t in others:
-        for h in range(n_section):
-            arrived(q_got.at[t, h], q_recv.at[t, h])
+        arrived(q_got.at[t, 0], q_recv.at[t, 0])
+        arrived(q_got.at[t, rest], q_recv.at[t, 1])
     for h in range(n_section):
         place = (h + n_section - s) % n_section
-        value = q_part[place, s].astype(jnp.float32)
+        value = q_part[s, place].astype(jnp.float32)
         for t in others:
-            value = value + q_got[t, h].astype(jnp.float32)
+            value = value + q_got[t, (h + n_section - t) % n_section].astype(jnp.float32)
         queries[h * BLOCK : (h + 1) * BLOCK, :] = turned(value * scaling).astype(jnp.bfloat16)
 
     first = ids_ref[0]
@@ -502,39 +509,51 @@
         acc[:, head : 2 * head] = acc[:, head : 2 * head] * factors + gained[:, head : 2 * head]
 
     def pass_on(i):
-        seq = ((z + i) % n_line) * 2 + c
-        for k, t in enumerate([direct, corner]):
-            number = seq * n_section + t
-            await_key(number)
-            hand_key(number, twin_send.at[i, k + 2], s, twin)
+        place = (z + i) % n_line
+        seq = place * 2 + c
+        for t in (direct, corner):
+            await_key(seq * n_section + t)
+        keys = plane(key_blocks, seq)
+        push(keys, keys, twin_send.at[i], key_twin_recv.at[place], s, twin)
         if i > 0:
-            for t in range(n_section):
-                number = seq * n_section + t
-                await_value(number)
-                hand_value(number, value_twin_send.at[i, t], s, twin)
+            values = plane(value_blocks, seq)
+            arrived(values, value_line_recv.at[place])
+            push(values, values, value_twin_send.at[i], value_twin_recv.at[place], s, twin)
 
     pass_on(0)
     for i in range(n_line):
         if i + 1 < n_line:
             pass_on(i + 1)
         place = (z + i) % n_line
-        for t in range(n_section):
-            number = (place * 2 + 1 - c) * n_section + t
-            await_key(number)
-            await_value(number)
+        seq = place * 2 + 1 - c
+        arrived(plane(key_blocks, seq), key_twin_recv.at[place])
+        arrived(plane(value_blocks, seq), value_twin_recv.at[place])
         attend(place)
 
     for h in range(n_section):
-        columns = pl.ds(h * head, head)
-        out_ref[s, :, columns] = (
-            acc[h * BLOCK : (h + 1) * BLOCK, 0:head] / acc[h * BLOCK : (h + 1) * BLOCK, head : 2 * head]
+        rows = pl.ds(h * BLOCK, BLOCK)
+        attended[s, :, h * head : (h + 1) * head] = (
+            acc[rows, 0:head] / acc[rows, head : 2 * head]
         ).astype(jnp.bfloat16)
-        piece = out_ref.at[s, :, columns]
-        for k, t in enumerate(others):
-            push(piece, piece, out_send.at[h, k], out_recv.at[s, h], t, j)
-    for t in others:
-        for h in range(n_section):
-            arrived(out_ref.at[t, :, pl.ds(h * head, head)], out_recv.at[t, h])
+    for k, t in enumerate(others):
+        push(attended.at[s], attended.at[s], out_send.at[k], out_recv.at[s], t, j)
+    get_o.wait()
+
+    def finish(owner, k):
+        rows = pl.ds(pl.multiple_of(owner * BLOCK, BLOCK), BLOCK)
+        result[rows, :] = jnp.dot(
+            attended[owner], wo[...], preferred_element_type=jnp.float32
+        ).astype(jnp.bfloat16)
+        copy = pltpu.make_async_copy(result.at[rows, :], out_ref.at[rows, :], store_sem.at[k])
+        copy.start()
+        return copy
+
+    stores = [finish(s, 0)]
+    for k, t in enumerate([across, along, corner]):
+        arrived(attended.at[t], out_recv.at[t])
+        stores.append(finish(t, k + 1))
+    for copy in stores:
+        copy.wait()
     for copy in pending:
         copy.wait_send()
 
@@ -561,11 +580,11 @@
     dma = pltpu.SemaphoreType.DMA
     bf16 = jnp.bfloat16
     f32 = jnp.float32
-    attended = pl.pallas_call(
+    return pl.pallas_call(
         functools.partial(fused, n_section, n_line),
-        out_shape=jax.ShapeDtypeStruct((n_section, BLOCK, n_section * head), bf16),
-        in_specs=[anywhere, vmem, anywhere, anywhere, anywhere, smem, smem],
-        out_specs=vmem,
+        out_shape=jax.ShapeDtypeStruct((rows, width), bf16),
+        in_specs=[anywhere, vmem, anywhere, anywhere, anywhere, anywhere, smem, smem],
+        out_specs=anywhere,
         scratch_shapes=[
             pltpu.VMEM((rows, width), bf16),
             pltpu.VMEM((rows, width), bf16),
@@ -585,6 +604,9 @@
             pltpu.VMEM((n_section * BLOCK, 2 * head), f32),
             pltpu.VMEM((n_section * BLOCK, 2 * n_section * BLOCK), f32),
             pltpu.VMEM((n_section * BLOCK, 2 * n_section * BLOCK), bf16),
+            pltpu.VMEM((n_section, BLOCK, n_section * head), bf16),
+            pltpu.VMEM((n_section * head, width), bf16),
+            pltpu.VMEM((rows, width), bf16),
             dma((5,)),
             dma((n_section,)),
             dma((n_section - 1,)),
@@ -597,18 +619,22 @@
             dma((n_section,)),
             dma((n_section - 1,)),
             dma((n_section,)),
-            dma((n_section, n_section - 1)),
-            dma((n_section, n_section)),
+            dma((2, n_section - 1)),
+            dma((n_section, 2)),
             dma((n_line - 1,)),
             dma((n_line, n_section - 1)),
-            dma((n_line, n_section)),
+            dma((n_line,)),
             dma((n_blocks,)),
+            dma((n_line,)),
             dma((n_section - 1,)),
-            dma((n_section, n_line - 1)),
-            dma((n_line, n_section)),
-            dma((n_blocks,)),
-            dma((n_section, n_section - 1)),
-            dma((n_section, n_section)),
+            dma((n_line - 1,)),
+            dma((n_line,)),
+            dma((n_section,)),
+            dma((n_line,)),
+            dma((n_line,)),
+            dma((n_section - 1,)),
+            dma((n_section,)),
+            dma((n_section,)),
         ],
         compiler_params=pltpu.CompilerParams(
             collective_id=0, has_side_effects=True, vmem_limit_bytes=60 * 1024 * 1024
@@ -619,13 +645,10 @@
         query_weight,
         key_weight,
         value_weight,
+        output_weight,
         block_reach,
         header_ids,
     )
-    return jnp.dot(
-        attended.reshape(rows, n_section * head), output_weight, preferred_element_type=f32
-    ).astype(bf16)
-
 
 def solution(mesh):
     n_section, n_seq = mesh.shape["section"], mesh.shape["seq"]

time: 51.4 us -> 50.9 us (level)
  matrix products: 2.73 us -> 0 us
  local copies, waits for them, and re-layouts: 0.01 us -> 2.26 us
    dot_general x1 -> x0, matrix products: 2.73 us -> none  [on_device_fused(): jnp.dot(attended.reshape(rows, n_section * head), output_weight, preferre...]
    unnamed x2 -> x1, local copies, waits for them, and re-layouts: 0.01 us -> 2.26 us
where the time goes in v6:
time: 50.9 us; the launch traced here: 50.8 us
  Pallas kernels  48.5 us (95%)
  local copies, waits for them, and re-layouts  2.26 us (4%)
    pallas_call x1, Pallas kernels, on_device_fused(): pl.pallas_call(functools.partial(fused, n_section, n_line), out_shape=jax...  48.5 us
    unnamed x1, local copies, waits for them, and re-layouts  2.26 us

profile of v6, /device:TPU:0, one launch (start us, length us, event | category | flops | bytes accessed | tf_op | source)
XLA Modules:
  0.0 50.8 jit_solution(17064426389565899972)
XLA Ops:
  0.0 48.5 %shard_map.82 = bf16[512,1024]{1,0:T(8,128)(2,1)} custom-call(bf16[512,1024]{1,0:T(8,128)(2,1)} %hidden_ref.1, bf16[1024]{0:T(1024)(128)(2,1)} %gain_ref.1, bf16[4096,128]{1,0:T(8,128)(2,1)} %query_ref.1, bf16[1024,128]{1,0:T(8,128)(2,1)} %key_ref.1, bf16[1024,128]{1,0:T(8,128)(2,1)} %value_ref.1, bf16[512,1024]{1,0:T(8,128)(2,1)} %project_ref.1, ...), custom_call_target="tpu_custom_call" | custom-call | tf_op jit(solution)/shard_map/pallas_call | solution.py:583
  48.5 2.3 %copy.10 = bf16[512,1024]{1,0:T(8,128)(2,1)} copy(bf16[512,1024]{1,0:T(8,128)(2,1)} %shard_map.82) | data formatting | bytes 2097152

commit v7 on v6

--- a/solution.py
+++ b/solution.py
@@ -399,8 +399,7 @@
     across = s + 1 - 2 * (s % 2)
     along = (s + 2) % n_section
     corner = (across + 2) % n_section
-    relayed = jnp.where(c == 0, across, along)
-    direct = jnp.where(c == 0, along, across)
+    peers = [across, along, corner]
 
     def hand_key(number, send, section, seq):
         piece = key_blocks.at[number]
@@ -420,23 +419,15 @@
         return blocks.at[pl.ds(seq * n_section, n_section)]
 
     def spread_key(number, slot):
-        hand_key(number, plane_send.at[slot, 0], relayed, j)
-        hand_key(number, plane_send.at[slot, 1], direct, j)
-
-    def relay_key(slot, seq):
-        number = seq * n_section + relayed
-        await_key(number)
-        hand_key(number, plane_send.at[slot, 2], direct, j)
+        for k, t in enumerate(peers):
+            hand_key(number, plane_send.at[slot, k], t, j)
 
     for k, i in enumerate(line):
         hand_key(b, line_send.at[k], s, i)
-    hand_value(b, value_plane_send.at[0], relayed)
-    hand_value(b, value_plane_send.at[1], direct)
+    for k, t in enumerate(peers):
+        hand_value(b, value_plane_send.at[k], t)
     spread_key(b, 0)
 
-    number = j * n_section + relayed
-    await_value(number)
-    hand_value(number, value_plane_send.at[2], direct)
     for k, t in enumerate(others):
         arrived(wq.at[t, far, :], wz_recv.at[t])
         push(wq.at[t, mine, :], wq.at[t, mine, :], wf_send.at[k], wf_recv.at[t], s, twin)
@@ -444,8 +435,8 @@
         number = i * n_section + s
         await_key(number)
         spread_key(number, k + 1)
-    await_value(j * n_section + direct)
-    await_value(j * n_section + corner)
+    for t in peers:
+        await_value(j * n_section + t)
     whole = plane(value_blocks, j)
     for k, i in enumerate(line):
         push(whole, whole, value_line_send.at[k], value_line_recv.at[z], s, i)
@@ -457,10 +448,6 @@
     rest = pl.ds(1, n_section - 1)
     for k, t in enumerate(others):
         push(q_part.at[t, rest], q_got.at[s, rest], q_send.at[1, k], q_recv.at[s, 1], t, j)
-    relay_key(0, j)
-    for k, i in enumerate(line):
-        relay_key(k + 1, i)
-
     for t in others:
         arrived(q_got.at[t, 0], q_recv.at[t, 0])
         arrived(q_got.at[t, rest], q_recv.at[t, 1])
@@ -483,14 +470,17 @@
     ones = jnp.ones((keys_wide, head), jnp.bfloat16)
     strip = 32
 
-    def attend(place):
+    def attend(place, low, high):
         start = place * group
         numbers = start + lax.broadcasted_iota(jnp.int32, (1, keys_wide), 1) // BLOCK
         valid = (numbers == first) | (numbers == second) | (jnp.abs(numbers - b) <= limit)
         bias = jnp.where(valid, 0.0, LOW)
         keys = jnp.concatenate([key_blocks[start + n] for n in range(group)], axis=1)
-        scores[...] = jnp.dot(queries[...], keys, preferred_element_type=jnp.float32)
-        for r in range(0, n_section * BLOCK, strip):
+        part_rows = pl.ds(low, high - low)
+        scores[part_rows, :] = jnp.dot(
+            queries[part_rows, :], keys, preferred_element_type=jnp.float32
+        )
+        for r in range(low, high, strip):
             rows = pl.ds(r, strip)
             part = scores[rows, :] * factor + bias
             before = top[rows, :]
@@ -500,18 +490,20 @@
             top[rows, :] = after
         values = value_blocks[pl.ds(start, group)].reshape(keys_wide, head)
         gained = jnp.dot(
-            weights[...],
+            weights[part_rows, :],
             jnp.concatenate([values, ones], axis=1),
             preferred_element_type=jnp.float32,
         )
-        factors = fade[...]
-        acc[:, 0:head] = acc[:, 0:head] * factors + gained[:, 0:head]
-        acc[:, head : 2 * head] = acc[:, head : 2 * head] * factors + gained[:, head : 2 * head]
+        factors = fade[part_rows, :]
+        for columns in (pl.ds(0, head), pl.ds(head, head)):
+            acc[part_rows, columns] = (
+                acc[part_rows, columns] * factors + gained[:, columns.start : columns.start + head]
+            )
 
     def pass_on(i):
         place = (z + i) % n_line
         seq = place * 2 + c
-        for t in (direct, corner):
+        for t in peers:
             await_key(seq * n_section + t)
         keys = plane(key_blocks, seq)
         push(keys, keys, twin_send.at[i], key_twin_recv.at[place], s, twin)
@@ -528,29 +520,37 @@
         seq = place * 2 + 1 - c
         arrived(plane(key_blocks, seq), key_twin_recv.at[place])
         arrived(plane(value_blocks, seq), value_twin_recv.at[place])
-        attend(place)
-
-    for h in range(n_section):
-        rows = pl.ds(h * BLOCK, BLOCK)
-        attended[s, :, h * head : (h + 1) * head] = (
-            acc[rows, 0:head] / acc[rows, head : 2 * head]
-        ).astype(jnp.bfloat16)
-    for k, t in enumerate(others):
-        push(attended.at[s], attended.at[s], out_send.at[k], out_recv.at[s], t, j)
+        if i + 1 < n_line:
+            attend(place, 0, n_section * BLOCK)
+    middle = n_section // 2
+    for m in range(2):
+        heads = range(m * middle, (m + 1) * middle)
+        attend(place, heads[0] * BLOCK, (heads[-1] + 1) * BLOCK)
+        for h in heads:
+            rows = pl.ds(h * BLOCK, BLOCK)
+            attended[s, m, :, (h - heads[0]) * head : (h - heads[0] + 1) * head] = (
+                acc[rows, 0:head] / acc[rows, head : 2 * head]
+            ).astype(jnp.bfloat16)
+        piece = attended.at[s, m]
+        for k, t in enumerate(others):
+            push(piece, piece, out_send.at[m, k], out_recv.at[s, m], t, j)
     get_o.wait()
 
     def finish(owner, k):
         rows = pl.ds(pl.multiple_of(owner * BLOCK, BLOCK), BLOCK)
         result[rows, :] = jnp.dot(
-            attended[owner], wo[...], preferred_element_type=jnp.float32
+            jnp.concatenate([attended[owner, 0], attended[owner, 1]], axis=1),
+            wo[...],
+            preferred_element_type=jnp.float32
         ).astype(jnp.bfloat16)
         copy = pltpu.make_async_copy(result.at[rows, :], out_ref.at[rows, :], store_sem.at[k])
         copy.start()
         return copy
 
     stores = [finish(s, 0)]
-    for k, t in enumerate([across, along, corner]):
-        arrived(attended.at[t], out_recv.at[t])
+    for k, t in enumerate(peers):
+        for m in range(2):
+            arrived(attended.at[t, m], out_recv.at[t, m])
         stores.append(finish(t, k + 1))
     for copy in stores:
         copy.wait()
@@ -604,7 +604,7 @@
             pltpu.VMEM((n_section * BLOCK, 2 * head), f32),
             pltpu.VMEM((n_section * BLOCK, 2 * n_section * BLOCK), f32),
             pltpu.VMEM((n_section * BLOCK, 2 * n_section * BLOCK), bf16),
-            pltpu.VMEM((n_section, BLOCK, n_section * head), bf16),
+            pltpu.VMEM((n_section, 2, BLOCK, n_section // 2 * head), bf16),
             pltpu.VMEM((n_section * head, width), bf16),
             pltpu.VMEM((rows, width), bf16),
             dma((5,)),
@@ -632,8 +632,8 @@
             dma((n_section,)),
             dma((n_line,)),
             dma((n_line,)),
-            dma((n_section - 1,)),
-            dma((n_section,)),
+            dma((2, n_section - 1)),
+            dma((n_section, 2)),
             dma((n_section,)),
         ],
         compiler_params=pltpu.CompilerParams(

time: 50.9 us -> 48.6 us (0.955)
  Pallas kernels: 48.5 us -> 46.2 us
    pallas_call x1, Pallas kernels: 48.5 us -> 46.2 us  [on_device_fused(): pl.pallas_call(functools.partial(fused, n_section, n_line), out_shape=jax...]
where the time goes in v7:
time: 48.6 us; the launch traced here: 48.5 us
  Pallas kernels  46.2 us (95%)
  local copies, waits for them, and re-layouts  2.26 us (5%)
    pallas_call x1, Pallas kernels, on_device_fused(): pl.pallas_call(functools.partial(fused, n_section, n_line), out_shape=jax...  46.2 us
    unnamed x1, local copies, waits for them, and re-layouts  2.26 us

profile of v7, /device:TPU:0, one launch (start us, length us, event | category | flops | bytes accessed | tf_op | source)
XLA Modules:
  0.0 48.5 jit_solution(1035552578503954843)
XLA Ops:
  0.0 46.2 %shard_map.82 = bf16[512,1024]{1,0:T(8,128)(2,1)} custom-call(bf16[512,1024]{1,0:T(8,128)(2,1)} %hidden_ref.1, bf16[1024]{0:T(1024)(128)(2,1)} %gain_ref.1, bf16[4096,128]{1,0:T(8,128)(2,1)} %query_ref.1, bf16[1024,128]{1,0:T(8,128)(2,1)} %key_ref.1, bf16[1024,128]{1,0:T(8,128)(2,1)} %value_ref.1, bf16[512,1024]{1,0:T(8,128)(2,1)} %project_ref.1, ...), custom_call_target="tpu_custom_call" | custom-call | tf_op jit(solution)/shard_map/pallas_call | solution.py:583
  46.2 2.3 %copy.10 = bf16[512,1024]{1,0:T(8,128)(2,1)} copy(bf16[512,1024]{1,0:T(8,128)(2,1)} %shard_map.82) | data formatting | bytes 2097152

commit v8 on v7

--- a/solution.py
+++ b/solution.py
@@ -514,8 +514,9 @@
 
     pass_on(0)
     for i in range(n_line):
-        if i + 1 < n_line:
-            pass_on(i + 1)
+        if i == 1:
+            for later in range(1, n_line):
+                pass_on(later)
         place = (z + i) % n_line
         seq = place * 2 + 1 - c
         arrived(plane(key_blocks, seq), key_twin_recv.at[place])

time: 48.6 us -> 48.8 us (level)
  no operation moved by 1% of the time
where the time goes in v8:
time: 48.8 us; the launch traced here: 48.6 us
  Pallas kernels  46.4 us (95%)
  local copies, waits for them, and re-layouts  2.26 us (5%)
    pallas_call x1, Pallas kernels, on_device_fused(): pl.pallas_call(functools.partial(fused, n_section, n_line), out_shape=jax...  46.4 us
    unnamed x1, local copies, waits for them, and re-layouts  2.26 us

profile of v8, /device:TPU:0, one launch (start us, length us, event | category | flops | bytes accessed | tf_op | source)
XLA Modules:
  0.0 48.6 jit_solution(150749484624522867)
XLA Ops:
  0.0 46.4 %shard_map.82 = bf16[512,1024]{1,0:T(8,128)(2,1)} custom-call(bf16[512,1024]{1,0:T(8,128)(2,1)} %hidden_ref.1, bf16[1024]{0:T(1024)(128)(2,1)} %gain_ref.1, bf16[4096,128]{1,0:T(8,128)(2,1)} %query_ref.1, bf16[1024,128]{1,0:T(8,128)(2,1)} %key_ref.1, bf16[1024,128]{1,0:T(8,128)(2,1)} %value_ref.1, bf16[512,1024]{1,0:T(8,128)(2,1)} %project_ref.1, ...), custom_call_target="tpu_custom_call" | custom-call | tf_op jit(solution)/shard_map/pallas_call | solution.py:584
  46.4 2.3 %copy.10 = bf16[512,1024]{1,0:T(8,128)(2,1)} copy(bf16[512,1024]{1,0:T(8,128)(2,1)} %shard_map.82) | data formatting | bytes 2097152
